TPU v7x, 256 devices: a whole 4x4x8 slice. The times are simulated.
256 devices in a mesh: wide: 32 (over x, z), pencil: 8 (over y, core).
Axes of the slice: x: 4, y: 4, z: 8, core: 2. Of those that a mesh axis runs over, the one named last changes fastest.
Arguments:
- force_adjoint: float32 [3, 8, 524288], P(None, 'pencil', 'wide'), may hold values from -4 to 4
- paint_index: int32 [8, 524288], P('pencil', 'wide'), may hold values from 0 to 511
- block_count: int32 [8, 1024], P('pencil', 'wide'), may hold values from 1 to 512, 314572 in all within a row
- block_owner: int32 [8, 1024, 1], P('pencil', 'wide'), may hold values from 0 to 31; in each aligned block of 32 rows (0 to 31, 32 to 63, ..., all dimensions but the last counted through in order) at most 2 rows name the same one
- block_tile: int32 [8, 1024], P('pencil', 'wide'), may hold values from 0 to 127
Outputs:
- mesh_grad: float32 [256, 256, 256], P('wide', 'pencil')
- mass_grad: float32 [8, 524288], P('pencil', 'wide')
Inputs may be any that keep to these rules, and one draw needn't show every extreme that they name: `block_owner`: no device sends more than 2 of its blocks to one owner, and some device sends exactly 2. `block_count`: the live particles of a block are its first slots.
All inputs are finite; a program needn't handle non-finite values.
Results may differ from a plain program's by a relative error of at most 0.00011.
Values sent between devices are 32-bit elements; how exact they have to be, the bound alone decides.
A program may use at most 64 MiB of HBM per device.

v0:
```python
import functools
import math

import jax
import jax.numpy as jnp
import ml_dtypes
import numpy as np
from jax import lax
from jax.experimental import pallas as pl
from jax.experimental.pallas import tpu as pltpu
from jax.sharding import PartitionSpec as P

NG = 256
NW = 32
NP = 8
NB = 32
BP = 512
MESH = pl.DeviceIdType.MESH
f32 = jnp.float32
bf16 = jnp.bfloat16


def roll(x, shift, axis):
    return pltpu.roll(x, shift, axis)


def halves(table):
    table = np.asarray(table, np.float32)
    high = table.astype(ml_dtypes.bfloat16)
    low = (table - high.astype(np.float32)).astype(ml_dtypes.bfloat16)
    return np.stack([high, low])


def waves(first, second):
    phase = (np.asarray(first)[:, None] * np.asarray(second)[None, :]) % NG
    angle = phase * (2.0 * math.pi / NG)
    return np.cos(angle), np.sin(angle)


def ky_of_row():
    out = []
    for w in range(NW):
        for j in range(8):
            base = 4 * w + j % 4
            out.append(base if j < 4 else (128 if base == 0 else NG - base))
    return np.array(out)


def make_tables():
    line = np.arange(NG)
    half = np.arange(NG // 2)
    sign = np.where(line % 2 == 0, 1.0, -1.0)
    c, s = waves(line, half)
    s = -s
    s[:, 0] = sign
    z_fwd = np.concatenate([c, s], axis=1)
    c, s = waves(half, line)
    weight = np.where(half == 0, 1.0, 2.0)[:, None]
    c = c * weight
    s = -2.0 * s
    s[0] = sign
    z_inv = np.concatenate([c, s], axis=0)
    ky = ky_of_row()
    c, s = waves(ky, line)
    y_fwd = np.concatenate([c, s], axis=0)
    kyt = ky.reshape(NW, 8).T.reshape(-1)
    c, s = waves(line, kyt)
    y_inv = np.concatenate([c, s], axis=0)
    xt = line.reshape(NW, 8).T.reshape(-1)
    c, s = waves(line, xt)
    x_fwd = np.concatenate([c, s], axis=0)
    c, s = waves(line, line)
    x_inv = np.concatenate([c, s], axis=0)
    return dict(
        z_fwd=halves(z_fwd),
        z_inv=halves(z_inv),
        z_inv_t=halves(z_inv.T),
        y_fwd=halves(y_fwd),
        y_inv=halves(y_inv),
        x_fwd=halves(x_fwd),
        x_inv=halves(x_inv),
    )


def dot(a, b, dims=((1,), (0,))):
    return lax.dot_general(a, b, (dims, ((), ())), preferred_element_type=f32)


def split(x):
    high = x.astype(bf16)
    return high, (x - high.astype(f32)).astype(bf16)


def dot3(a, b, dims=((1,), (0,))):
    return dot(a[0], b[0], dims) + (dot(a[0], b[1], dims) + dot(a[1], b[0], dims))


def iota(shape, axis):
    return lax.broadcasted_iota(jnp.int32, shape, axis)


def exchange(arrays):
    chunk = iota(arrays[0].shape, 1) // 16
    for b in range(3):
        bit = (chunk >> b) & 1
        new = []
        for i in range(8):
            mine = (i >> b) & 1
            shift = 16 << b if mine == 0 else 128 - (16 << b)
            new.append(jnp.where(bit == mine, arrays[i], roll(arrays[i ^ (1 << b)], shift, 1)))
        arrays = new
    return arrays


def one_hot_rows(ids):
    spot = (ids & 31) * 8 + iota((NW, 8, 128), 1)
    spot = spot.reshape(NW * 8, 128)
    lane = iota((NW * 8, 128), 1)
    both = jnp.concatenate(
        [jnp.where(spot == lane, 1.0, 0.0), jnp.where(spot == lane + 128, 1.0, 0.0)], axis=1
    )
    return both.astype(bf16)


def tile_y(ids):
    return jnp.broadcast_to(ids >> 5, (NW, 8, 128)).reshape(NW * 8, 128)


def scatter_rows(field, ty0, ty1):
    upper = (iota((NW * 8, 128), 1) >= 64).astype(jnp.int32)
    turned = roll(field, 64, 1)
    first = jnp.where(upper == 0, field, turned)
    second = jnp.where(upper == 0, turned, field)
    rows = []
    for values, ty in ((first, ty0), (second, ty1)):
        rows.append(
            jnp.concatenate(
                [jnp.where(ty == upper, values, 0.0), jnp.where(ty == upper + 2, values, 0.0)],
                axis=1,
            )
        )
    return jnp.concatenate(rows, axis=0)


def pick_rows(v0, v1, ty0, ty1):
    lower = iota((NW * 8, 128), 1) < 64
    out = []
    for v, ty in ((v0, ty0), (v1, ty1)):
        half = jnp.where(ty >= 2, v[:, 128:], v[:, :128])
        out.append((half, roll(half, 64, 1)))
    first = jnp.where((ty0 & 1) == 1, out[0][1], out[0][0])
    second = jnp.where((ty1 & 1) == 1, out[1][0], out[1][1])
    return jnp.where(lower, first, second)


def y_slopes():
    row = iota((NG, 128), 0)
    base = (row >> 3) * 4 + (row & 3)
    return jnp.where((row & 4) == 0, base, -base).astype(f32)


def y_forward(table, real, imag):
    out = dot3(table, split(jnp.concatenate([real, imag], axis=1)))
    return out[:NG, :128] + out[NG:, 128:], out[:NG, 128:] - out[NG:, :128]


def back(table, real, imag):
    out = dot3(table, split(jnp.concatenate([real, imag], axis=1)))
    return out[:NG, :128] - out[NG:, 128:], out[:NG, 128:] + out[NG:, :128]


def solve_x(x_fwd, x_inv, first, second, w, p):
    a = dot3(x_fwd, split(first))
    b = dot3(x_fwd, split(second))
    cra, cia, sra, sia = a[:NG, :128], a[:NG, 128:], a[NG:, :128], a[NG:, 128:]
    crb, cib, srb, sib = b[:NG, :128], b[:NG, 128:], b[NG:, :128], b[NG:, 128:]
    row = iota((NG, 128), 0)
    lane = iota((NG, 128), 1)
    signed = jnp.where(row < 128, row, row - NG)
    slope = jnp.where(row == 128, 0, signed).astype(f32)
    p_re = slope * (cra + sia) + (crb + sib)
    p_im = slope * (cia - sra) + (cib - srb)
    q_re = (crb - sib) - slope * (cra - sia)
    q_im = slope * (cia + sra) - (cib + srb)
    alone = (w == 0) & ((lane & 63) < 16)
    r_re = jnp.where(alone, q_re, roll(q_re, 64, 1))
    r_im = jnp.where(alone, q_im, roll(q_im, 64, 1))
    j = lane >> 4
    base = 4 * w + (j & 3)
    ny = jnp.where((base == 0) & (j == 4), 128, base)
    kz = lane & 15
    nz = 16 * p + kz
    flat = signed * signed + ny * ny
    factor = (1.0 / NG**2) / jnp.maximum(flat + nz * nz, 1).astype(f32)
    top = (1.0 / NG**2) / (flat + (NG // 2) ** 2).astype(f32)
    shared = (nz == 0)
    alpha = jnp.where(shared, 0.5 * (factor + top), factor)
    beta = jnp.where(shared, 0.5 * (top - factor), 0.0)
    h_re = -(alpha * p_im + beta * r_im)
    h_im = alpha * p_re + beta * r_re
    return back(x_inv, h_re, h_im)


def block_key(cells_ref, b, slot):
    cells = cells_ref[0:1, pl.ds(pl.multiple_of(b * BP, BP), BP)]
    key = (cells >> 3) + 64 * slot
    spread = jnp.where(iota((128, BP), 0) == key, 1.0, 0.0).astype(bf16)
    return spread, cells & 7


def paint_kernel(count_ref, owner_ref, tile_ref, force_ref, cells_ref, msg_ref, ids_ref, seen):
    msg_ref[...] = jnp.zeros_like(msg_ref)
    ids_ref[...] = jnp.full(ids_ref.shape, -1, jnp.int32)
    for o in range(NW):
        seen[o] = 0

    def body(b, carry):
        owner = owner_ref[0, b]
        slot = seen[owner]
        seen[owner] = slot + 1
        ids_ref[owner, slot] = jnp.full((1, 128), tile_ref[0, b], jnp.int32)
        spread, cz = block_key(cells_ref, b, slot)
        live = iota((1, BP), 1) < count_ref[0, b]
        keep = (iota((8, BP), 0) == cz) & live
        high, low = [], []
        for f in range(3):
            amount = force_ref[f, 0:1, pl.ds(pl.multiple_of(b * BP, BP), BP)]
            top = amount.astype(bf16).astype(f32)
            high.append(jnp.where(keep, top, 0.0))
            low.append(jnp.where(keep, amount - top, 0.0))
        left = jnp.concatenate(high + low, axis=0).astype(bf16)
        out = dot(left, spread, ((1,), (1,)))
        msg_ref[owner] += (out[:24] + out[24:]).reshape(3, 8, 128)
        return carry

    lax.fori_loop(0, NB, body, 0, unroll=4)


def read_kernel(count_ref, owner_ref, cells_ref, ret_ref, mass_ref, seen):
    for o in range(NW):
        seen[o] = 0

    def body(b, carry):
        owner = owner_ref[0, b]
        slot = seen[owner]
        seen[owner] = slot + 1
        spread, cz = block_key(cells_ref, b, slot)
        live = iota((1, BP), 1) < count_ref[0, b]
        keep = (iota((8, BP), 0) == cz) & live
        tile = ret_ref[pl.ds(pl.multiple_of(owner * 8, 8), 8), :]
        top = tile.astype(bf16).astype(f32)
        left = jnp.concatenate([top, tile - top], axis=0).astype(bf16)
        out = dot(left, spread)
        value = jnp.sum(jnp.where(keep, out[:8] + out[8:], 0.0), axis=0, keepdims=True)
        mass_ref[0:1, pl.ds(pl.multiple_of(b * BP, BP), BP)] = value
        return carry

    lax.fori_loop(0, NB, body, 0, unroll=4)


def mesh_kernel(
    msg_ref, ids_ref, z_fwd, z_inv, z_inv_t, y_fwd, y_inv, x_fwd, x_inv,
    mesh_ref, ret_ref,
    ids_rx, msg_rx, snd2, rx2, snd3, rx3, snd4, rx4, snd5, rx5, snd6,
    wsend, wrecv, psend, precv, lsem,
):
    w = lax.axis_index("wide")
    p = lax.axis_index("pencil")

    barrier = pltpu.get_barrier_semaphore()

    def greet_wide(d, carry):
        pl.semaphore_signal(barrier, inc=1, device_id={"wide": (w + d) % NW}, device_id_type=MESH)
        return carry

    def greet_pencil(d, carry):
        pl.semaphore_signal(barrier, inc=1, device_id={"pencil": (p + d) % NP}, device_id_type=MESH)
        return carry

    lax.fori_loop(1, NW, greet_wide, 0)
    lax.fori_loop(1, NP, greet_pencil, 0)
    pl.semaphore_wait(barrier, NW - 1 + NP - 1)

    def wide_copy(phase, src, dst, other):
        return pltpu.make_async_remote_copy(
            src_ref=src, dst_ref=dst, send_sem=wsend.at[phase, other], recv_sem=wrecv.at[phase, w],
            device_id={"wide": other}, device_id_type=MESH,
        )

    def wide_send(phase, src, dst):
        def step(d, carry):
            other = (w + d) % NW
            wide_copy(phase, src(other), dst(w), other).start()
            return carry

        lax.fori_loop(1, NW, step, 0)

    def wide_wait(phase, src, dst):
        def step(d, carry):
            other = (w + d) % NW
            pltpu.make_async_remote_copy(
                src_ref=src(other), dst_ref=dst(other), send_sem=wsend.at[phase, other],
                recv_sem=wrecv.at[phase, other], device_id={"wide": other}, device_id_type=MESH,
            ).wait()
            return carry

        lax.fori_loop(1, NW, step, 0)

    def pencil_send(phase, src, dst):
        def step(d, carry):
            other = (p + d) % NP
            pltpu.make_async_remote_copy(
                src_ref=src(other), dst_ref=dst(p), send_sem=psend.at[phase, other],
                recv_sem=precv.at[phase, p], device_id={"pencil": other}, device_id_type=MESH,
            ).start()
            return carry

        lax.fori_loop(1, NP, step, 0)

    def pencil_wait(phase, src, dst):
        def step(d, carry):
            other = (p + d) % NP
            pltpu.make_async_remote_copy(
                src_ref=src(other), dst_ref=dst(other), send_sem=psend.at[phase, other],
                recv_sem=precv.at[phase, other], device_id={"pencil": other}, device_id_type=MESH,
            ).wait()
            return carry

        lax.fori_loop(1, NP, step, 0)

    def keep_own(src, dst):
        copy = pltpu.make_async_copy(src, dst, lsem)
        copy.start()
        copy.wait()

    def rows8(ref, i):
        return ref.at[:, pl.ds(pl.multiple_of(i * 8, 8), 8), :]

    def rows32(ref, i):
        return ref.at[:, pl.ds(pl.multiple_of(i * 32, 32), 32), :]

    id_src, id_dst = (lambda i: ids_ref.at[i]), (lambda i: ids_rx.at[i])
    msg_src, msg_dst = (lambda i: msg_ref.at[i]), (lambda i: msg_rx.at[i])
    wide_send(0, id_src, id_dst)
    wide_send(1, msg_src, msg_dst)
    keep_own(ids_ref.at[w], ids_rx.at[w])
    keep_own(msg_ref.at[w], msg_rx.at[w])
    wide_wait(0, id_src, id_dst)
    ids0, ids1 = ids_rx[:, 0], ids_rx[:, 1]
    chosen = jnp.concatenate([one_hot_rows(ids0), one_hot_rows(ids1)], axis=0)
    g_fwd = [dot(chosen, z_fwd[i]).astype(bf16) for i in range(2)]
    g_inv = [dot(chosen, z_inv_t[i]).astype(bf16) for i in range(2)]
    ty0, ty1 = tile_y(ids0), tile_y(ids1)
    wide_wait(1, msg_src, msg_dst)

    kz = (iota((NG, 256), 1) & 127).astype(f32)
    for f in range(3):
        field = msg_rx[:, f].reshape(NW * 8, 128)
        placed = split(scatter_rows(field, ty0, ty1))
        lines = dot3(placed, g_fwd, ((0,), (0,)))
        if f == 2:
            lines = lines * kz
        for c in range(2):
            part = lines[:, c * 128 : (c + 1) * 128]
            by_x = [
                jnp.concatenate(
                    [part[ty * 64 + cx * 8 : ty * 64 + cx * 8 + 8] for ty in range(4)], axis=0
                )
                for cx in range(8)
            ]
            for i, value in enumerate(exchange(by_x)):
                snd2[f, c, 32 * i : 32 * i + 32, :] = value
        s, r = snd2.at[f], rx2.at[f]
        pencil_send(f, functools.partial(rows32, s), functools.partial(rows32, r))
    for f in range(3):
        keep_own(rows32(snd2.at[f], p), rows32(rx2.at[f], p))

    slope = y_slopes()
    parts = []
    table = (y_fwd[0], y_fwd[1])
    for f in range(3):
        s, r = snd2.at[f], rx2.at[f]
        pencil_wait(f, functools.partial(rows32, s), functools.partial(rows32, r))
        real, imag = y_forward(table, rx2[f, 0], rx2[f, 1])
        if f == 0:
            snd3[0, 0], snd3[0, 1] = real, imag
            s, r = snd3.at[0], rx3.at[0]
            wide_send(2, functools.partial(rows8, s), functools.partial(rows8, r))
        elif f == 1:
            snd3[1, 0], snd3[1, 1] = slope * real, slope * imag
        else:
            snd3[1, 0] += real
            snd3[1, 1] += imag
            s, r = snd3.at[1], rx3.at[1]
            wide_send(3, functools.partial(rows8, s), functools.partial(rows8, r))
    for i in range(2):
        keep_own(rows8(snd3.at[i], w), rows8(rx3.at[i], w))

    both = []
    for i in range(2):
        s, r = snd3.at[i], rx3.at[i]
        wide_wait(2 + i, functools.partial(rows8, s), functools.partial(rows8, r))
        both.append(
            jnp.concatenate(
                [
                    jnp.concatenate(
                        exchange([rx3[i, c, pl.ds(j, NW, stride=8), :] for j in range(8)]), axis=0
                    )
                    for c in range(2)
                ],
                axis=1,
            )
        )
    real, imag = solve_x(
        (x_fwd[0], x_fwd[1]), (x_inv[0], x_inv[1]), both[0], both[1], w, p
    )
    snd4[0], snd4[1] = real, imag
    s4, d4 = functools.partial(rows8, snd4), functools.partial(rows8, rx4)
    wide_send(4, s4, d4)
    keep_own(rows8(snd4, w), rows8(rx4, w))
    wide_wait(4, s4, d4)

    parts = [
        jnp.concatenate(exchange([rx4[c, pl.ds(j, NW, stride=8), :] for j in range(8)]), axis=0)
        for c in range(2)
    ]
    real, imag = back((y_inv[0], y_inv[1]), parts[0], parts[1])
    snd5[0], snd5[1] = real, imag
    s5, d5 = functools.partial(rows32, snd5), functools.partial(rows32, rx5)
    pencil_send(3, s5, d5)
    keep_own(rows32(snd5, p), rows32(rx5, p))
    pencil_wait(3, s5, d5)

    halves_z = []
    for c in range(2):
        by_x = exchange([rx5[c, 32 * i : 32 * i + 32, :] for i in range(8)])
        halves_z.append(
            jnp.concatenate(
                [by_x[cx][ty * 8 : ty * 8 + 8] for ty in range(4) for cx in range(8)], axis=0
            )
        )
    lines = split(jnp.concatenate(halves_z, axis=1))
    values = dot3(g_inv, lines, ((1,), (1,)))
    snd6[...] = pick_rows(values[: NW * 8], values[NW * 8 :], ty0, ty1)

    def row8(ref, i):
        return ref.at[pl.ds(pl.multiple_of(i * 8, 8), 8), :]

    s6, d6 = functools.partial(row8, snd6), functools.partial(row8, ret_ref)
    wide_send(5, s6, d6)
    keep_own(row8(snd6, w), row8(ret_ref, w))
    mesh = dot3(lines, (z_inv[0], z_inv[1]))
    for ty in range(4):
        for cx in range(8):
            mesh_ref[cx, ty * 8 : ty * 8 + 8, :] = mesh[ty * 64 + cx * 8 : ty * 64 + cx * 8 + 8]
    wide_wait(5, s6, d6)


def on_device(force_adjoint, paint_index, block_count, block_owner, block_tile):
    owner = block_owner.reshape(1, NB)
    smem = pl.BlockSpec(memory_space=pltpu.SMEM)
    vmem = pl.BlockSpec(memory_space=pltpu.VMEM)
    msg, ids = pl.pallas_call(
        paint_kernel,
        out_shape=(
            jax.ShapeDtypeStruct((NW, 3, 8, 128), f32),
            jax.ShapeDtypeStruct((NW, 2, 1, 128), jnp.int32),
        ),
        in_specs=[smem] * 3 + [vmem] * 2,
        out_specs=(vmem, vmem),
        scratch_shapes=[pltpu.SMEM((NW,), jnp.int32)],
        compiler_params=pltpu.CompilerParams(vmem_limit_bytes=32 << 20),
        name="paint",
    )(block_count, owner, block_tile, force_adjoint, paint_index)

    tabs = make_tables()
    names = ["z_fwd", "z_inv", "z_inv_t", "y_fwd", "y_inv", "x_fwd", "x_inv"]
    mesh_grad, ret = pl.pallas_call(
        mesh_kernel,
        out_shape=(
            jax.ShapeDtypeStruct((8, 32, NG), f32),
            jax.ShapeDtypeStruct((NG, 128), f32),
        ),
        in_specs=[vmem] * (2 + len(names)),
        out_specs=(vmem, vmem),
        scratch_shapes=[
            pltpu.VMEM((NW, 2, 1, 128), jnp.int32),
            pltpu.VMEM((NW, 3, 8, 128), f32),
            pltpu.VMEM((3, 2, NG, 128), f32),
            pltpu.VMEM((3, 2, NG, 128), f32),
            pltpu.VMEM((2, 2, NG, 128), f32),
            pltpu.VMEM((2, 2, NG, 128), f32),
            pltpu.VMEM((2, NG, 128), f32),
            pltpu.VMEM((2, NG, 128), f32),
            pltpu.VMEM((2, NG, 128), f32),
            pltpu.VMEM((2, NG, 128), f32),
            pltpu.VMEM((NG, 128), f32),
            pltpu.SemaphoreType.DMA((6, NW)),
            pltpu.SemaphoreType.DMA((6, NW)),
            pltpu.SemaphoreType.DMA((4, NP)),
            pltpu.SemaphoreType.DMA((4, NP)),
            pltpu.SemaphoreType.DMA,
        ],
        compiler_params=pltpu.CompilerParams(
            collective_id=0, has_side_effects=True, vmem_limit_bytes=48 << 20
        ),
        name="mesh",
    )(msg, ids, *[jnp.asarray(tabs[n]) for n in names])

    mass_grad = pl.pallas_call(
        read_kernel,
        out_shape=jax.ShapeDtypeStruct((1, NB * BP), f32),
        in_specs=[smem] * 2 + [vmem] * 2,
        out_specs=vmem,
        scratch_shapes=[pltpu.SMEM((NW,), jnp.int32)],
        compiler_params=pltpu.CompilerParams(vmem_limit_bytes=32 << 20),
        name="read",
    )(block_count, owner, paint_index, ret)
    return mesh_grad, mass_grad


def solution(mesh):
    return jax.shard_map(
        on_device,
        mesh=mesh,
        in_specs=(
            P(None, "pencil", "wide"),
            P("pencil", "wide"),
            P("pencil", "wide"),
            P("pencil", "wide", None),
            P("pencil", "wide"),
        ),
        out_specs=(P("wide", "pencil", None), P("pencil", "wide")),
        check_vma=False,
    )
```

profile of v0, /device:TPU:1, one launch (start us, length us, event | category | flops | bytes accessed | tf_op | source)
XLA Modules:
  0.0 93.8 jit_solution(4613172157879977839)
XLA Ops:
  0.6 0.0 copy-start.4
  0.6 0.0 copy-start.7
  0.7 0.9 copy-done.7
  1.5 0.0 copy-start.9
  1.5 0.9 copy-done.9
  2.5 0.0 copy-start.10
  2.5 0.7 copy-done.10
  3.1 0.0 copy-start.12
  3.1 0.7 copy-done.12
  3.8 0.7 copy-done.14
  4.4 3.1 %paint.1 = (f32[32,3,8,128]{3,2,1,0:T(8,128)S(1)}, s32[32,2,1,128]{3,2,1,0:T(1,128)S(1)}) custom-call(s32[1,32]{1,0:T(1,128)S(1)} %copy-done.10, s32[1,32]{1,0:T(1,128)S(1)} %bitcast.1, s32[1,32]{1,0:T(1,128)S(1)} %copy-done.14, f32[3,1,16384]{2,1,0:T(1,128)S(1)} %copy-done.9, s32[1,16384]{1,0:T(1,128)S(1)} %copy-done.7), custom_call_target="tpu_custom_call" | custom-call | tf_op jit(solution)/shard_map/paint/pallas_call | solution.py:463
  7.5 0.0 copy-done.4
  7.5 0.0 copy-start
  7.6 1.0 %copy-done = bf16[2,512,256]{2,1,0:T(8,128)(2,1)S(1)} copy-done((bf16[2,512,256]{2,1,0:T(8,128)(2,1)S(1)}, bf16[2,512,256]{2,1,0:T(8,128)(2,1)}, u32[]{:S(2)}) %copy-start) | copy-done | bytes 524312
  8.6 0.0 copy-start.1
  8.6 1.0 %copy-done.1 = bf16[2,512,256]{2,1,0:T(8,128)(2,1)S(1)} copy-done((bf16[2,512,256]{2,1,0:T(8,128)(2,1)S(1)}, bf16[2,512,256]{2,1,0:T(8,128)(2,1)}, u32[]{:S(2)}) %copy-start.1) | copy-done | bytes 524312
  9.6 0.0 copy-start.2
  9.6 1.0 %copy-done.2 = bf16[2,512,256]{2,1,0:T(8,128)(2,1)S(1)} copy-done((bf16[2,512,256]{2,1,0:T(8,128)(2,1)S(1)}, bf16[2,512,256]{2,1,0:T(8,128)(2,1)}, u32[]{:S(2)}) %copy-start.2) | copy-done | bytes 524312
  10.7 0.0 copy-start.3
  10.7 1.0 %copy-done.3 = bf16[2,512,256]{2,1,0:T(8,128)(2,1)S(1)} copy-done((bf16[2,512,256]{2,1,0:T(8,128)(2,1)S(1)}, bf16[2,512,256]{2,1,0:T(8,128)(2,1)}, u32[]{:S(2)}) %copy-start.3) | copy-done | bytes 524312
  11.7 0.0 copy-start.5
  11.7 0.9 %copy-done.5 = bf16[2,256,256]{2,1,0:T(8,128)(2,1)S(1)} copy-done((bf16[2,256,256]{2,1,0:T(8,128)(2,1)S(1)}, bf16[2,256,256]{2,1,0:T(8,128)(2,1)}, u32[]{:S(2)}) %copy-start.5) | copy-done | bytes 262168
  12.7 0.9 %copy-done.6 = bf16[2,256,256]{2,1,0:T(8,128)(2,1)S(1)} copy-done((bf16[2,256,256]{2,1,0:T(8,128)(2,1)S(1)}, bf16[2,256,256]{2,1,0:T(8,128)(2,1)}, u32[]{:S(2)}) %copy-start.6) | copy-done | bytes 262168
  13.6 0.0 copy-start.8
  13.6 75.8 %mesh.1 = (f32[8,32,256]{2,1,0:T(8,128)S(1)}, f32[256,128]{1,0:T(8,128)S(1)}) custom-call(f32[32,3,8,128]{3,2,1,0:T(8,128)S(1)} %get-tuple-element.6.msg_ref, s32[32,2,1,128]{3,2,1,0:T(1,128)S(1)} %get-tuple-element.7.ids_ref, bf16[2,256,256]{2,1,0:T(8,128)(2,1)S(1)} %copy-done.6, bf16[2,256,256]{2,1,0:T(8,128)(2,1)S(1)} %copy-done.5, ...), custom_call_target="tpu_custom_call" | custom-call | tf_op jit(solution)/shard_map/mesh/pallas_call | solution.py:478
  89.4 0.0 copy-start.11
  89.4 0.0 copy-start.13
  89.5 0.0 copy-done.8
  89.5 0.6 copy-done.11
  90.1 0.0 copy-done.13
  90.1 3.0 %read.1 = f32[1,16384]{1,0:T(1,128)} custom-call(s32[1,32]{1,0:T(1,128)S(1)} %copy-done.11, s32[1,32]{1,0:T(1,128)S(1)} %bitcast.2, s32[1,16384]{1,0:T(1,128)S(1)} %copy-done.8, f32[256,128]{1,0:T(8,128)S(1)} %get-tuple-element.9.ret_ref), custom_call_target="tpu_custom_call" | custom-call | tf_op jit(solution)/shard_map/read/pallas_call | solution.py:510
  93.1 0.7 copy.15
  (2 shorter events, 0.0 us)
Async XLA Ops:
  0.6 6.9 %copy-start.4 = (bf16[2,256,256]{2,1,0:T(8,128)(2,1)S(1)}, bf16[2,256,256]{2,1,0:T(8,128)(2,1)}, u32[]{:S(2)}) copy-start(bf16[2,256,256]{2,1,0:T(8,128)(2,1)} %constant.16.clone.z_inv_t) | copy-start | bytes 786436
  0.6 0.9 copy-start.7
  1.5 0.9 copy-start.9
  2.5 0.7 copy-start.10
  3.1 0.7 copy-start.12
  3.8 0.7 copy-start.14
  7.5 1.0 %copy-start = (bf16[2,512,256]{2,1,0:T(8,128)(2,1)S(1)}, bf16[2,512,256]{2,1,0:T(8,128)(2,1)}, u32[]{:S(2)}) copy-start(bf16[2,512,256]{2,1,0:T(8,128)(2,1)} %constant.20.clone.x_inv) | copy-start | bytes 1572868
  8.6 1.0 %copy-start.1 = (bf16[2,512,256]{2,1,0:T(8,128)(2,1)S(1)}, bf16[2,512,256]{2,1,0:T(8,128)(2,1)}, u32[]{:S(2)}) copy-start(bf16[2,512,256]{2,1,0:T(8,128)(2,1)} %constant.19.clone.x_fwd) | copy-start | bytes 1572868
  9.6 1.0 %copy-start.2 = (bf16[2,512,256]{2,1,0:T(8,128)(2,1)S(1)}, bf16[2,512,256]{2,1,0:T(8,128)(2,1)}, u32[]{:S(2)}) copy-start(bf16[2,512,256]{2,1,0:T(8,128)(2,1)} %constant.18.clone.y_inv) | copy-start | bytes 1572868
  10.7 1.0 %copy-start.3 = (bf16[2,512,256]{2,1,0:T(8,128)(2,1)S(1)}, bf16[2,512,256]{2,1,0:T(8,128)(2,1)}, u32[]{:S(2)}) copy-start(bf16[2,512,256]{2,1,0:T(8,128)(2,1)} %constant.17.clone.y_fwd) | copy-start | bytes 1572868
  11.7 0.9 %copy-start.5 = (bf16[2,256,256]{2,1,0:T(8,128)(2,1)S(1)}, bf16[2,256,256]{2,1,0:T(8,128)(2,1)}, u32[]{:S(2)}) copy-start(bf16[2,256,256]{2,1,0:T(8,128)(2,1)} %constant.15.clone.z_inv) | copy-start | bytes 786436
  12.7 0.9 %copy-start.6 = (bf16[2,256,256]{2,1,0:T(8,128)(2,1)S(1)}, bf16[2,256,256]{2,1,0:T(8,128)(2,1)}, u32[]{:S(2)}) copy-start(bf16[2,256,256]{2,1,0:T(8,128)(2,1)} %constant.14.clone.z_fwd) | copy-start | bytes 786436
  13.6 75.8 %copy-start.8 = (s32[1,16384]{1,0:T(1,128)S(1)}, s32[1,16384]{1,0:T(1,128)}, u32[]{:S(2)}) copy-start(s32[1,16384]{1,0:T(1,128)} %cells_ref.3) | copy-start | bytes 196612
  89.4 0.7 copy-start.11
  89.4 0.7 copy-start.13
where the time goes:
time: 94.2 us; the launch traced here: 93.8 us
  Pallas kernels  81.9 us (87%)
  local copies, waits for them, and re-layouts  11.2 us (12%)
    pallas_call x1, Pallas kernels, on_device(): pl.pallas_call(mesh_kernel, out_shape=(jax.ShapeDtypeStruct((8, 32, NG),...  75.8 us
    unnamed x31, local copies, waits for them, and re-layouts  11.2 us
    pallas_call x1, Pallas kernels, on_device(): pl.pallas_call(paint_kernel, out_shape=(jax.ShapeDtypeStruct((NW, 3, 8, 1...  3.1 us
    pallas_call x1, Pallas kernels, on_device(): pl.pallas_call(read_kernel, out_shape=jax.ShapeDtypeStruct((1, NB * BP),...  3.02 us

commit v1 on v0

v1 whole, which is shorter than its diff:
```python
import math

import jax
import jax.numpy as jnp
import ml_dtypes
import numpy as np
from jax import lax
from jax.experimental import pallas as pl
from jax.experimental.pallas import tpu as pltpu
from jax.sharding import PartitionSpec as P

NG = 256
NW = 32
NP = 8
NB = 32
BP = 512
MESH = pl.DeviceIdType.MESH
f32 = jnp.float32
bf16 = jnp.bfloat16


def roll(x, shift, axis):
    return pltpu.roll(x, shift, axis)


def halves(table):
    table = np.asarray(table, np.float32)
    high = table.astype(ml_dtypes.bfloat16)
    low = (table - high.astype(np.float32)).astype(ml_dtypes.bfloat16)
    return np.stack([high, low])


def waves(first, second):
    phase = (np.asarray(first)[:, None] * np.asarray(second)[None, :]) % NG
    angle = phase * (2.0 * math.pi / NG)
    return np.cos(angle), np.sin(angle)


def ky_of_row():
    out = []
    for w in range(NW):
        for j in range(8):
            base = 4 * w + j % 4
            out.append(base if j < 4 else (128 if base == 0 else NG - base))
    return np.array(out)


def make_tables():
    line = np.arange(NG)
    half = np.arange(NG // 2)
    sign = np.where(line % 2 == 0, 1.0, -1.0)
    c, s = waves(line, half)
    s = -s
    s[:, 0] = sign
    z_fwd = np.concatenate([c, s], axis=1)
    c, s = waves(half, line)
    weight = np.where(half == 0, 1.0, 2.0)[:, None]
    c = c * weight
    s = -2.0 * s
    s[0] = sign
    z_inv = np.concatenate([c, s], axis=0)
    ky = ky_of_row()
    c, s = waves(ky, line)
    y_fwd = np.concatenate([c, s], axis=0)
    kyt = ky.reshape(NW, 8).T.reshape(-1)
    c, s = waves(line, kyt)
    y_inv = np.concatenate([c, s], axis=0)
    xt = line.reshape(NW, 8).T.reshape(-1)
    c, s = waves(line, xt)
    x_fwd = np.concatenate([c, s], axis=0)
    c, s = waves(line, line)
    x_inv = np.concatenate([c, s], axis=0)
    return dict(
        z_fwd=halves(z_fwd),
        z_inv=halves(z_inv),
        z_inv_t=halves(z_inv.T),
        y_fwd=halves(y_fwd),
        y_inv=halves(y_inv),
        x_fwd=halves(x_fwd),
        x_inv=halves(x_inv),
    )


def dot(a, b, dims=((1,), (0,))):
    return lax.dot_general(a, b, (dims, ((), ())), preferred_element_type=f32)


def split(x):
    high = x.astype(bf16)
    return high, (x - high.astype(f32)).astype(bf16)


def dot3(a, b, dims=((1,), (0,))):
    return dot(a[0], b[0], dims) + (dot(a[0], b[1], dims) + dot(a[1], b[0], dims))


def iota(shape, axis):
    return lax.broadcasted_iota(jnp.int32, shape, axis)


def exchange(arrays):
    chunk = iota(arrays[0].shape, 1) // 16
    for b in range(3):
        bit = (chunk >> b) & 1
        new = []
        for i in range(8):
            mine = (i >> b) & 1
            shift = 16 << b if mine == 0 else 128 - (16 << b)
            new.append(jnp.where(bit == mine, arrays[i], roll(arrays[i ^ (1 << b)], shift, 1)))
        arrays = new
    return arrays


def one_hot_rows(ids):
    spot = (ids & 31) * 8 + iota((NW, 8, 128), 1)
    spot = spot.reshape(NW * 8, 128)
    lane = iota((NW * 8, 128), 1)
    both = jnp.concatenate(
        [jnp.where(spot == lane, 1.0, 0.0), jnp.where(spot == lane + 128, 1.0, 0.0)], axis=1
    )
    return both.astype(bf16)


def tile_y(ids):
    return jnp.broadcast_to(ids >> 5, (NW, 8, 128)).reshape(NW * 8, 128)


def scatter_rows(field, ty0, ty1):
    upper = (iota((NW * 8, 128), 1) >= 64).astype(jnp.int32)
    turned = roll(field, 64, 1)
    first = jnp.where(upper == 0, field, turned)
    second = jnp.where(upper == 0, turned, field)
    rows = []
    for values, ty in ((first, ty0), (second, ty1)):
        rows.append(
            jnp.concatenate(
                [jnp.where(ty == upper, values, 0.0), jnp.where(ty == upper + 2, values, 0.0)],
                axis=1,
            )
        )
    return jnp.concatenate(rows, axis=0)


def pick_rows(v0, v1, ty0, ty1):
    lower = iota((NW * 8, 128), 1) < 64
    out = []
    for v, ty in ((v0, ty0), (v1, ty1)):
        half = jnp.where(ty >= 2, v[:, 128:], v[:, :128])
        out.append((half, roll(half, 64, 1)))
    first = jnp.where((ty0 & 1) == 1, out[0][1], out[0][0])
    second = jnp.where((ty1 & 1) == 1, out[1][0], out[1][1])
    return jnp.where(lower, first, second)


def y_slopes():
    row = iota((NG, 128), 0)
    base = (row >> 3) * 4 + (row & 3)
    return jnp.where((row & 4) == 0, base, -base).astype(f32)


def y_forward(table, real, imag):
    out = dot3(table, split(jnp.concatenate([real, imag], axis=1)))
    return out[:NG, :128] + out[NG:, 128:], out[:NG, 128:] - out[NG:, :128]


def back(table, real, imag):
    out = dot3(table, split(jnp.concatenate([real, imag], axis=1)))
    return out[:NG, :128] - out[NG:, 128:], out[:NG, 128:] + out[NG:, :128]


def solve_x(x_inv, a, b, w, p):
    cra, cia, sra, sia = a[:NG, :128], a[:NG, 128:], a[NG:, :128], a[NG:, 128:]
    crb, cib, srb, sib = b[:NG, :128], b[:NG, 128:], b[NG:, :128], b[NG:, 128:]
    row = iota((NG, 128), 0)
    lane = iota((NG, 128), 1)
    signed = jnp.where(row < 128, row, row - NG)
    slope = jnp.where(row == 128, 0, signed).astype(f32)
    p_re = slope * (cra + sia) + (crb + sib)
    p_im = slope * (cia - sra) + (cib - srb)
    q_re = (crb - sib) - slope * (cra - sia)
    q_im = slope * (cia + sra) - (cib + srb)
    alone = (w == 0) & ((lane & 63) < 16)
    r_re = jnp.where(alone, q_re, roll(q_re, 64, 1))
    r_im = jnp.where(alone, q_im, roll(q_im, 64, 1))
    j = lane >> 4
    base = 4 * w + (j & 3)
    ny = jnp.where((base == 0) & (j == 4), 128, base)
    kz = lane & 15
    nz = 16 * p + kz
    flat = signed * signed + ny * ny
    factor = (1.0 / NG**2) / jnp.maximum(flat + nz * nz, 1).astype(f32)
    top = (1.0 / NG**2) / (flat + (NG // 2) ** 2).astype(f32)
    shared = (nz == 0)
    alpha = jnp.where(shared, 0.5 * (factor + top), factor)
    beta = jnp.where(shared, 0.5 * (top - factor), 0.0)
    h_re = -(alpha * p_im + beta * r_im)
    h_im = alpha * p_re + beta * r_re
    return back(x_inv, h_re, h_im)


def wide_peer(w, i):
    iz, ix = i // 4, i % 4
    dz = 4 + (iz + 1) // 2 * (1 - 2 * ((iz + 1) % 2))
    dx = 2 + (ix + 1) // 2 * (1 - 2 * ((ix + 1) % 2))
    return (w // 8 + dx) % 4 * 8 + (w + dz) % 8


def loop(count, step, unroll=1):
    def body(i, carry):
        step(i)
        return carry

    lax.fori_loop(0, count, body, 0, unroll=unroll)


def rows(ref, i, size):
    return ref.at[:, pl.ds(pl.multiple_of(i * size, 8), size), :]


def step_kernel(
    force_hbm, cells_hbm, count_hbm, owner_hbm, tile_hbm,
    z_fwd_hbm, z_inv_t_hbm, z_inv_hbm, y_fwd_hbm, y_inv_hbm, x_fwd_hbm, x_inv_hbm,
    mesh_ref, mass_ref,
    force, cells, count, owner, tile, owner_v,
    z_fwd, z_inv_t, z_inv, y_fwd, y_inv, x_fwd, x_inv,
    spread, tiles, pick_v, pick, ids, msg, ids_rx, msg_rx,
    snd2, rx2, snd3, rx3, snd4, rx4, snd5, rx5, snd6, rx6,
    arg_sem, table_sem, pick_sem, wide_out, wide_in, pencil_out, pencil_in,
):
    w = lax.axis_index("wide")
    p = lax.axis_index("pencil")

    arg_copies = [
        pltpu.make_async_copy(src, dst, arg_sem.at[i])
        for i, (src, dst) in enumerate(
            [
                (owner_hbm, owner_v), (owner_hbm, owner), (count_hbm, count), (tile_hbm, tile),
                (cells_hbm, cells), (force_hbm, force),
            ]
        )
    ]
    table_copies = [
        pltpu.make_async_copy(src, dst, table_sem.at[i])
        for i, (src, dst) in enumerate(
            [
                (z_fwd_hbm, z_fwd), (z_inv_t_hbm, z_inv_t), (y_fwd_hbm, y_fwd),
                (x_fwd_hbm, x_fwd), (x_inv_hbm, x_inv), (y_inv_hbm, y_inv), (z_inv_hbm, z_inv),
            ]
        )
    ]
    for copy in arg_copies:
        copy.start()
    barrier = pltpu.get_barrier_semaphore()
    loop(
        NW - 1,
        lambda i: pl.semaphore_signal(
            barrier, inc=1, device_id={"wide": wide_peer(w, i)}, device_id_type=MESH
        ),
    )
    loop(
        NP - 1,
        lambda i: pl.semaphore_signal(
            barrier, inc=1, device_id={"pencil": (p + 1 + i) % NP}, device_id_type=MESH
        ),
    )
    for copy in table_copies:
        copy.start()

    def wide_copy(phase, src, dst, other):
        return pltpu.make_async_remote_copy(
            src_ref=src, dst_ref=dst, send_sem=wide_out.at[phase], recv_sem=wide_in.at[phase],
            device_id={"wide": other}, device_id_type=MESH,
        )

    def pencil_copy(phase, src, dst, other):
        return pltpu.make_async_remote_copy(
            src_ref=src, dst_ref=dst, send_sem=pencil_out.at[phase], recv_sem=pencil_in.at[phase],
            device_id={"pencil": other}, device_id_type=MESH,
        )

    def wide_send(phase, src, dst):
        def step(i):
            other = wide_peer(w, i)
            wide_copy(phase, rows(src, other, 8), rows(dst, w, 8), other).start()

        loop(NW - 1, step)
        here = pl.ds(pl.multiple_of(w * 8, 8), 8)
        dst[:, here, :] = src[:, here, :]

    def wide_all(phase, src, dst):
        part = pl.ds(0, (NW - 1) * 8)
        return wide_copy(phase, src.at[:, part, :], dst.at[:, part, :], (w + 1) % NW)

    def pencil_send(phase, src, dst):
        def step(i):
            other = (p + 1 + i) % NP
            pencil_copy(phase, rows(src, other, 32), rows(dst, p, 32), other).start()

        loop(NP - 1, step)
        here = pl.ds(pl.multiple_of(p * 32, 32), 32)
        dst[:, here, :] = src[:, here, :]

    def pencil_all(phase, src, dst):
        part = pl.ds(0, (NP - 1) * 32)
        return pencil_copy(phase, src.at[:, part, :], dst.at[:, part, :], (p + 1) % NP)

    arg_copies[0].wait()
    block = iota((NW, NB), 1)
    match = owner_v[...] == iota((NW, NB), 0)
    first = jnp.min(jnp.where(match, block, NB), axis=1, keepdims=True)
    last = jnp.max(jnp.where(match, block, -1), axis=1, keepdims=True)
    second = jnp.where(last > first, last, NB)
    pick_v[...] = jnp.where(iota((NW, 128), 1) == 0, first, second)
    pick_copy = pltpu.make_async_copy(pick_v, pick, pick_sem)
    pick_copy.start()

    for copy in arg_copies[1:]:
        copy.wait()
    tiles[NB] = jnp.zeros((3, 8, 128), f32)

    def slots(b):
        return pl.ds(pl.multiple_of(b * BP, BP), BP)

    def kept(b):
        live = iota((1, BP), 1) < count[0, b]
        return (iota((8, BP), 0) == (cells[0:1, slots(b)] & 7)) & live

    def paint(b):
        key = cells[0:1, slots(b)] >> 3
        hot = jnp.where((iota((128, BP), 0) & 63) == key, 1.0, 0.0).astype(bf16)
        spread[b] = hot
        keep = kept(b)
        high, low = [], []
        for f in range(3):
            amount = force[f, 0:1, slots(b)]
            top = amount.astype(bf16).astype(f32)
            high.append(jnp.where(keep, top, 0.0))
            low.append(jnp.where(keep, amount - top, 0.0))
        out = dot(jnp.concatenate(high + low, axis=0).astype(bf16), hot, ((1,), (1,)))
        tiles[b] = (out[:24] + out[24:]).reshape(3, 8, 128)

    loop(NB, paint, unroll=4)
    pick_copy.wait()
    pl.semaphore_wait(barrier, NW - 1 + NP - 1)

    left = iota((8, 128), 1) < 64

    def assemble(f, o):
        msg[f, o] = jnp.where(left, tiles[pick[o, 0], f], tiles[pick[o, 1], f])

    def number(o):
        for s in range(2):
            b = pick[o, s]
            t = jnp.where(b < NB, tile[0, jnp.minimum(b, NB - 1)], -1)
            ids[o, s] = jnp.full((1, 128), t, jnp.int32)

    def send_first(i):
        other = wide_peer(w, i)
        number(other)
        wide_copy(0, ids.at[other], ids_rx.at[w], other).start()
        assemble(0, other)
        wide_copy(1, msg.at[0, other], msg_rx.at[0, w], other).start()

    loop(NW - 1, send_first)
    for f in (1, 2):

        def send_field(i, f=f):
            other = wide_peer(w, i)
            assemble(f, other)
            wide_copy(1 + f, msg.at[f, other], msg_rx.at[f, w], other).start()

        loop(NW - 1, send_field)
    number(w)
    ids_rx[w] = ids[w]
    for f in range(3):
        assemble(f, w)
        msg_rx[f, w] = msg[f, w]
    others = pl.ds(0, NW - 1)
    ids_all = wide_copy(0, ids.at[others], ids_rx.at[others], (w + 1) % NW)
    msg_all = [
        wide_copy(1 + f, msg.at[f, others], msg_rx.at[f, others], (w + 1) % NW) for f in range(3)
    ]
    ids_all.wait_recv()
    ids0, ids1 = ids_rx[:, 0], ids_rx[:, 1]
    chosen = jnp.concatenate([one_hot_rows(ids0), one_hot_rows(ids1)], axis=0)
    table_copies[0].wait()
    table_copies[1].wait()
    g_fwd = [dot(chosen, z_fwd[i]).astype(bf16) for i in range(2)]
    g_inv = [dot(chosen, z_inv_t[i]).astype(bf16) for i in range(2)]
    ty0, ty1 = tile_y(ids0), tile_y(ids1)

    kz = (iota((NG, 256), 1) & 127).astype(f32)
    for f in range(3):
        msg_all[f].wait_recv()
        field = msg_rx[f].reshape(NW * 8, 128)
        lines = dot3(split(scatter_rows(field, ty0, ty1)), g_fwd, ((0,), (0,)))
        if f == 2:
            lines = lines * kz
        for c in range(2):
            part = lines[:, c * 128 : (c + 1) * 128]
            by_x = [
                jnp.concatenate(
                    [part[ty * 64 + cx * 8 : ty * 64 + cx * 8 + 8] for ty in range(4)], axis=0
                )
                for cx in range(8)
            ]
            for i, value in enumerate(exchange(by_x)):
                snd2[f, c, 32 * i : 32 * i + 32, :] = value
        pencil_send(f, snd2.at[f], rx2.at[f])

    slope = y_slopes()
    table_copies[2].wait()
    for f in range(3):
        pencil_all(f, snd2.at[f], rx2.at[f]).wait_recv()
        real, imag = y_forward((y_fwd[0], y_fwd[1]), rx2[f, 0], rx2[f, 1])
        if f == 0:
            snd3[0, 0], snd3[0, 1] = real, imag
            wide_send(4, snd3.at[0], rx3.at[0])
        elif f == 1:
            snd3[1, 0], snd3[1, 1] = slope * real, slope * imag
        else:
            snd3[1, 0] += real
            snd3[1, 1] += imag
            wide_send(5, snd3.at[1], rx3.at[1])

    table_copies[3].wait()
    table_copies[4].wait()
    both = []
    for i in range(2):
        wide_all(4 + i, snd3.at[i], rx3.at[i]).wait_recv()
        parts = [
            jnp.concatenate(
                exchange([rx3[i, c, pl.ds(j, NW, stride=8), :] for j in range(8)]), axis=0
            )
            for c in range(2)
        ]
        both.append(dot3((x_fwd[0], x_fwd[1]), split(jnp.concatenate(parts, axis=1))))
    snd4[0], snd4[1] = solve_x((x_inv[0], x_inv[1]), both[0], both[1], w, p)
    wide_send(6, snd4, rx4)

    table_copies[5].wait()
    wide_all(6, snd4, rx4).wait_recv()
    parts = [
        jnp.concatenate(exchange([rx4[c, pl.ds(j, NW, stride=8), :] for j in range(8)]), axis=0)
        for c in range(2)
    ]
    snd5[0], snd5[1] = back((y_inv[0], y_inv[1]), parts[0], parts[1])
    pencil_send(3, snd5, rx5)

    table_copies[6].wait()
    pencil_all(3, snd5, rx5).wait_recv()
    halves_z = []
    for c in range(2):
        by_x = exchange([rx5[c, 32 * i : 32 * i + 32, :] for i in range(8)])
        halves_z.append(
            jnp.concatenate(
                [by_x[cx][ty * 8 : ty * 8 + 8] for ty in range(4) for cx in range(8)], axis=0
            )
        )
    lines = split(jnp.concatenate(halves_z, axis=1))
    values = dot3(g_inv, lines, ((1,), (1,)))
    snd6[...] = pick_rows(values[: NW * 8], values[NW * 8 :], ty0, ty1).reshape(NW, 8, 128)

    def send_back(i):
        other = wide_peer(w, i)
        wide_copy(7, snd6.at[other], rx6.at[w], other).start()

    loop(NW - 1, send_back)
    rx6[w] = snd6[w]
    mesh = dot3(lines, (z_inv[0], z_inv[1]))
    for ty in range(4):
        for cx in range(8):
            mesh_ref[cx, ty * 8 : ty * 8 + 8, :] = mesh[ty * 64 + cx * 8 : ty * 64 + cx * 8 + 8]
    ids_all.wait_send()
    for f in range(3):
        msg_all[f].wait_send()
        pencil_all(f, snd2.at[f], rx2.at[f]).wait_send()
    for i in range(2):
        wide_all(4 + i, snd3.at[i], rx3.at[i]).wait_send()
    wide_all(6, snd4, rx4).wait_send()
    pencil_all(3, snd5, rx5).wait_send()
    wide_copy(7, snd6.at[others], rx6.at[others], (w + 1) % NW).wait()

    lower = iota((8, 128), 1) < 64

    def read(b):
        o = owner[0, b]
        here = jnp.where(pick[o, 0] == b, 0, 1)
        tile_in = rx6[o]
        side = jnp.where(lower, 0, 1)
        tile_in = jnp.where(side == here, tile_in, 0.0)
        top = tile_in.astype(bf16).astype(f32)
        out = dot(jnp.concatenate([top, tile_in - top], axis=0).astype(bf16), spread[b])
        value = jnp.sum(jnp.where(kept(b), out[:8] + out[8:], 0.0), axis=0, keepdims=True)
        mass_ref[0:1, slots(b)] = value

    loop(NB, read, unroll=4)


def on_device(force_adjoint, paint_index, block_count, block_owner, block_tile):
    tabs = make_tables()
    names = ["z_fwd", "z_inv_t", "z_inv", "y_fwd", "y_inv", "x_fwd", "x_inv"]
    tables = [tabs[n] for n in names]
    vmem = pl.BlockSpec(memory_space=pltpu.VMEM)
    wave = pltpu.VMEM((2, NG, 128), f32)
    dma = pltpu.SemaphoreType.DMA
    mesh_grad, mass_grad = pl.pallas_call(
        step_kernel,
        out_shape=(
            jax.ShapeDtypeStruct((8, 32, NG), f32),
            jax.ShapeDtypeStruct((1, NB * BP), f32),
        ),
        in_specs=[pl.BlockSpec(memory_space=pl.ANY)] * (5 + len(names)),
        out_specs=(vmem, vmem),
        scratch_shapes=[
            pltpu.VMEM((3, 1, NB * BP), f32),
            pltpu.VMEM((1, NB * BP), jnp.int32),
            pltpu.SMEM((1, NB), jnp.int32),
            pltpu.SMEM((1, NB), jnp.int32),
            pltpu.SMEM((1, NB), jnp.int32),
            pltpu.VMEM((1, NB), jnp.int32),
            *[pltpu.VMEM(t.shape, bf16) for t in tables],
            pltpu.VMEM((NB, 128, BP), bf16),
            pltpu.VMEM((NB + 1, 3, 8, 128), f32),
            pltpu.VMEM((NW, 128), jnp.int32),
            pltpu.SMEM((NW, 128), jnp.int32),
            pltpu.VMEM((NW, 2, 1, 128), jnp.int32),
            pltpu.VMEM((3, NW, 8, 128), f32),
            pltpu.VMEM((NW, 2, 1, 128), jnp.int32),
            pltpu.VMEM((3, NW, 8, 128), f32),
            pltpu.VMEM((3, 2, NG, 128), f32),
            pltpu.VMEM((3, 2, NG, 128), f32),
            pltpu.VMEM((2, 2, NG, 128), f32),
            pltpu.VMEM((2, 2, NG, 128), f32),
            wave, wave, wave, wave,
            pltpu.VMEM((NW, 8, 128), f32),
            pltpu.VMEM((NW, 8, 128), f32),
            dma((6,)), dma((7,)), dma, dma((8,)), dma((8,)), dma((4,)), dma((4,)),
        ],
        compiler_params=pltpu.CompilerParams(
            collective_id=0, has_side_effects=True, vmem_limit_bytes=60 << 20
        ),
        name="step",
    )(
        force_adjoint, paint_index, block_count, block_owner.reshape(1, NB), block_tile,
        *[jnp.asarray(t) for t in tables],
    )
    return mesh_grad, mass_grad


def solution(mesh):
    return jax.shard_map(
        on_device,
        mesh=mesh,
        in_specs=(
            P(None, "pencil", "wide"),
            P("pencil", "wide"),
            P("pencil", "wide"),
            P("pencil", "wide", None),
            P("pencil", "wide"),
        ),
        out_specs=(P("wide", "pencil", None), P("pencil", "wide")),
        check_vma=False,
    )
```

time: 94.2 us -> 70.3 us (0.75)
  Pallas kernels: 81.9 us -> 67.2 us
  local copies, waits for them, and re-layouts: 11.2 us -> 2.34 us
    pallas_call x3 -> x1, Pallas kernels: 81.9 us -> 67.2 us  [on_device(): pl.pallas_call(step_kernel, out_shape=(jax.ShapeDtypeStruct((8, 32, NG),...]
    unnamed x31 -> x4, local copies, waits for them, and re-layouts: 11.2 us -> 2.34 us
where the time goes in v1:
time: 70.3 us; the launch traced here: 70.2 us
  Pallas kernels  67.2 us (96%)
  local copies, waits for them, and re-layouts  2.34 us (3%)
    pallas_call x1, Pallas kernels, on_device(): pl.pallas_call(step_kernel, out_shape=(jax.ShapeDtypeStruct((8, 32, NG),...  67.2 us
    unnamed x4, local copies, waits for them, and re-layouts  2.34 us

profile of v1, /device:TPU:1, one launch (start us, length us, event | category | flops | bytes accessed | tf_op | source)
XLA Modules:
  0.0 70.2 jit_solution(2970151669465603768)
XLA Ops:
  0.6 67.2 %step.1 = (f32[8,32,256]{2,1,0:T(8,128)}, f32[1,16384]{1,0:T(1,128)}) custom-call(f32[3,1,16384]{2,1,0:T(1,128)} %force_hbm.1, s32[1,16384]{1,0:T(1,128)} %cells_hbm.1, s32[1,32]{1,0:T(1,128)} %count_hbm.1, s32[1,32]{1,0:T(1,128)} %bitcast.1, s32[1,32]{1,0:T(1,128)} %tile_hbm.1, bf16[2,256,256]{2,1,0:T(8,128)(2,1)} %constant.14.clone.z_fwd_hbm, ...), custom_call_target="tpu_custom_call" | custom-call | tf_op jit(solution)/shard_map/step/pallas_call | solution.py:507
  67.8 0.0 copy-start
  67.9 1.7 %copy.16 = f32[8,32,256]{2,1,0:T(8,128)} copy(f32[8,32,256]{2,1,0:T(8,128)} %get-tuple-element.4) | data formatting | bytes 524288
  69.6 0.0 copy-done
  69.6 0.6 copy.17
Async XLA Ops:
  67.8 1.7 %copy-start = (f32[1,16384]{1,0:T(1,128)S(1)}, f32[1,16384]{1,0:T(1,128)}, u32[]{:S(2)}) copy-start(f32[1,16384]{1,0:T(1,128)} %get-tuple-element.5) | copy-start | bytes 196612

commit v2 on v1

--- a/solution.py
+++ b/solution.py
@@ -69,7 +69,8 @@
     c, s = waves(line, xt)
     x_fwd = np.concatenate([c, s], axis=0)
     c, s = waves(line, line)
-    x_inv = np.concatenate([c, s], axis=0)
+    full = np.stack([np.concatenate([c, -s], axis=1), np.concatenate([s, c], axis=1)])
+    x_inv = full.reshape(2, NW, 2, 4, 2 * NG).transpose(2, 1, 0, 3, 4).reshape(2 * NG, 2 * NG)
     return dict(
         z_fwd=halves(z_fwd),
         z_inv=halves(z_inv),
@@ -112,17 +113,12 @@
 
 
 def one_hot_rows(ids):
-    spot = (ids & 31) * 8 + iota((NW, 8, 128), 1)
-    spot = spot.reshape(NW * 8, 128)
+    spot = (ids & 31) * 8 + (iota((NW * 8, 128), 0) & 7)
     lane = iota((NW * 8, 128), 1)
     both = jnp.concatenate(
         [jnp.where(spot == lane, 1.0, 0.0), jnp.where(spot == lane + 128, 1.0, 0.0)], axis=1
     )
     return both.astype(bf16)
-
-
-def tile_y(ids):
-    return jnp.broadcast_to(ids >> 5, (NW, 8, 128)).reshape(NW * 8, 128)
 
 
 def scatter_rows(field, ty0, ty1):
@@ -158,17 +154,16 @@
     return jnp.where((row & 4) == 0, base, -base).astype(f32)
 
 
-def y_forward(table, real, imag):
-    out = dot3(table, split(jnp.concatenate([real, imag], axis=1)))
-    return out[:NG, :128] + out[NG:, 128:], out[:NG, 128:] - out[NG:, :128]
-
-
-def back(table, real, imag):
-    out = dot3(table, split(jnp.concatenate([real, imag], axis=1)))
-    return out[:NG, :128] - out[NG:, 128:], out[:NG, 128:] + out[NG:, :128]
-
-
-def solve_x(x_inv, a, b, w, p):
+def combine(sums, sign):
+    out = []
+    for k in range(0, sums.shape[1], 128):
+        turned = roll(sums[NG:, k : k + 128], 64, 1)
+        real = iota((NG, 128), 1) < 64
+        out.append(sums[:NG, k : k + 128] + jnp.where(real, -sign * turned, sign * turned))
+    return out
+
+
+def solve_x(a, b, w, p):
     cra, cia, sra, sia = a[:NG, :128], a[:NG, 128:], a[NG:, :128], a[NG:, 128:]
     crb, cib, srb, sib = b[:NG, :128], b[:NG, 128:], b[NG:, :128], b[NG:, 128:]
     row = iota((NG, 128), 0)
@@ -195,7 +190,7 @@
     beta = jnp.where(shared, 0.5 * (top - factor), 0.0)
     h_re = -(alpha * p_im + beta * r_im)
     h_im = alpha * p_re + beta * r_re
-    return back(x_inv, h_re, h_im)
+    return h_re, h_im
 
 
 def wide_peer(w, i):
@@ -205,12 +200,21 @@
     return (w // 8 + dx) % 4 * 8 + (w + dz) % 8
 
 
+def pencil_peer(p, i):
+    dy = 2 + (i // 2 + 1) // 2 * (1 - 2 * ((i // 2 + 1) % 2))
+    return (p // 2 + dy) % 4 * 2 + (p + i + i // 6) % 2
+
+
 def loop(count, step, unroll=1):
     def body(i, carry):
         step(i)
         return carry
 
     lax.fori_loop(0, count, body, 0, unroll=unroll)
+
+
+def half(ref, h):
+    return ref.at[pl.ds(h, 1)]
 
 
 def rows(ref, i, size):
@@ -224,7 +228,7 @@
     force, cells, count, owner, tile, owner_v,
     z_fwd, z_inv_t, z_inv, y_fwd, y_inv, x_fwd, x_inv,
     spread, tiles, pick_v, pick, ids, msg, ids_rx, msg_rx,
-    snd2, rx2, snd3, rx3, snd4, rx4, snd5, rx5, snd6, rx6,
+    snd2, rx2, snd3, rx3, snd4, rx4, snd5, rx5, snd6, rx6, mesh_v,
     arg_sem, table_sem, pick_sem, wide_out, wide_in, pencil_out, pencil_in,
 ):
     w = lax.axis_index("wide")
@@ -260,7 +264,7 @@
     loop(
         NP - 1,
         lambda i: pl.semaphore_signal(
-            barrier, inc=1, device_id={"pencil": (p + 1 + i) % NP}, device_id_type=MESH
+            barrier, inc=1, device_id={"pencil": pencil_peer(p, i)}, device_id_type=MESH
         ),
     )
     for copy in table_copies:
@@ -293,7 +297,7 @@
 
     def pencil_send(phase, src, dst):
         def step(i):
-            other = (p + 1 + i) % NP
+            other = pencil_peer(p, i)
             pencil_copy(phase, rows(src, other, 32), rows(dst, p, 32), other).start()
 
         loop(NP - 1, step)
@@ -327,7 +331,7 @@
 
     def paint(b):
         key = cells[0:1, slots(b)] >> 3
-        hot = jnp.where((iota((128, BP), 0) & 63) == key, 1.0, 0.0).astype(bf16)
+        hot = jnp.where(iota((64, BP), 0) == key, 1.0, 0.0).astype(bf16)
         spread[b] = hot
         keep = kept(b)
         high, low = [], []
@@ -337,7 +341,8 @@
             high.append(jnp.where(keep, top, 0.0))
             low.append(jnp.where(keep, amount - top, 0.0))
         out = dot(jnp.concatenate(high + low, axis=0).astype(bf16), hot, ((1,), (1,)))
-        tiles[b] = (out[:24] + out[24:]).reshape(3, 8, 128)
+        out = out[:24] + out[24:]
+        tiles[b] = jnp.concatenate([out, out], axis=1).reshape(3, 8, 128)
 
     loop(NB, paint, unroll=4)
     pick_copy.wait()
@@ -349,10 +354,11 @@
         msg[f, o] = jnp.where(left, tiles[pick[o, 0], f], tiles[pick[o, 1], f])
 
     def number(o):
+        name = []
         for s in range(2):
             b = pick[o, s]
-            t = jnp.where(b < NB, tile[0, jnp.minimum(b, NB - 1)], -1)
-            ids[o, s] = jnp.full((1, 128), t, jnp.int32)
+            name.append(jnp.where(b < NB, tile[0, jnp.minimum(b, NB - 1)], -1))
+        ids[o] = jnp.where(iota((1, 128), 1) < 64, name[0], name[1])
 
     def send_first(i):
         other = wide_peer(w, i)
@@ -381,13 +387,16 @@
         wide_copy(1 + f, msg.at[f, others], msg_rx.at[f, others], (w + 1) % NW) for f in range(3)
     ]
     ids_all.wait_recv()
-    ids0, ids1 = ids_rx[:, 0], ids_rx[:, 1]
+    pair = jnp.broadcast_to(ids_rx[...], (NW, 8, 128)).reshape(NW * 8, 128)
+    turned = roll(pair, 64, 1)
+    lower = iota((NW * 8, 128), 1) < 64
+    ids0, ids1 = jnp.where(lower, pair, turned), jnp.where(lower, turned, pair)
     chosen = jnp.concatenate([one_hot_rows(ids0), one_hot_rows(ids1)], axis=0)
     table_copies[0].wait()
     table_copies[1].wait()
     g_fwd = [dot(chosen, z_fwd[i]).astype(bf16) for i in range(2)]
     g_inv = [dot(chosen, z_inv_t[i]).astype(bf16) for i in range(2)]
-    ty0, ty1 = tile_y(ids0), tile_y(ids1)
+    ty0, ty1 = ids0 >> 5, ids1 >> 5
 
     kz = (iota((NG, 256), 1) & 127).astype(f32)
     for f in range(3):
@@ -396,105 +405,129 @@
         lines = dot3(split(scatter_rows(field, ty0, ty1)), g_fwd, ((0,), (0,)))
         if f == 2:
             lines = lines * kz
-        for c in range(2):
-            part = lines[:, c * 128 : (c + 1) * 128]
+        for h in range(2):
             by_x = [
                 jnp.concatenate(
-                    [part[ty * 64 + cx * 8 : ty * 64 + cx * 8 + 8] for ty in range(4)], axis=0
+                    [
+                        lines[ty * 64 + cx * 8 : ty * 64 + cx * 8 + 8, c * 128 : c * 128 + 128]
+                        for ty in range(4)
+                    ],
+                    axis=0,
                 )
-                for cx in range(8)
+                for c in range(2)
+                for cx in range(4 * h, 4 * h + 4)
             ]
             for i, value in enumerate(exchange(by_x)):
-                snd2[f, c, 32 * i : 32 * i + 32, :] = value
-        pencil_send(f, snd2.at[f], rx2.at[f])
+                snd2[f, h, 32 * i : 32 * i + 32, :] = value
+            if f == 2:
+                pencil_send(2 + h, half(snd2.at[f], h), half(rx2.at[f], h))
+        if f < 2:
+            pencil_send(f, snd2.at[f], rx2.at[f])
 
     slope = y_slopes()
     table_copies[2].wait()
-    for f in range(3):
+    for f in range(2):
         pencil_all(f, snd2.at[f], rx2.at[f]).wait_recv()
-        real, imag = y_forward((y_fwd[0], y_fwd[1]), rx2[f, 0], rx2[f, 1])
+        both = jnp.concatenate([rx2[f, 0], rx2[f, 1]], axis=1)
+        for h, value in enumerate(combine(dot3((y_fwd[0], y_fwd[1]), split(both)), -1.0)):
+            snd3[f, h] = value if f == 0 else slope * value
         if f == 0:
-            snd3[0, 0], snd3[0, 1] = real, imag
             wide_send(4, snd3.at[0], rx3.at[0])
-        elif f == 1:
-            snd3[1, 0], snd3[1, 1] = slope * real, slope * imag
-        else:
-            snd3[1, 0] += real
-            snd3[1, 1] += imag
-            wide_send(5, snd3.at[1], rx3.at[1])
+    for h in range(2):
+        pencil_all(2 + h, half(snd2.at[2], h), half(rx2.at[2], h)).wait_recv()
+        sums = dot3((y_fwd[0], y_fwd[1]), split(rx2[2, h]))
+        snd3[1, h] += combine(sums, -1.0)[0]
+        wide_send(5 + h, half(snd3.at[1], h), half(rx3.at[1], h))
 
     table_copies[3].wait()
     table_copies[4].wait()
-    both = []
-    for i in range(2):
-        wide_all(4 + i, snd3.at[i], rx3.at[i]).wait_recv()
-        parts = [
-            jnp.concatenate(
-                exchange([rx3[i, c, pl.ds(j, NW, stride=8), :] for j in range(8)]), axis=0
-            )
-            for c in range(2)
-        ]
-        both.append(dot3((x_fwd[0], x_fwd[1]), split(jnp.concatenate(parts, axis=1))))
-    snd4[0], snd4[1] = solve_x((x_inv[0], x_inv[1]), both[0], both[1], w, p)
-    wide_send(6, snd4, rx4)
+
+    def x_part(i, h):
+        parts = exchange([rx3[i, h, pl.ds(j, NW, stride=8), :] for j in range(8)])
+        parts = [jnp.concatenate(parts[c : c + 4], axis=0) for c in (0, 4)]
+        table = [x_fwd[k, :, h * 128 : h * 128 + 128] for k in range(2)]
+        return dot3(table, split(jnp.concatenate(parts, axis=1)))
+
+    wide_all(4, snd3.at[0], rx3.at[0]).wait_recv()
+    first = x_part(0, 0) + x_part(0, 1)
+    second = []
+    for h in range(2):
+        wide_all(5 + h, half(snd3.at[1], h), half(rx3.at[1], h)).wait_recv()
+        second.append(x_part(1, h))
+    spectrum = split(jnp.concatenate(solve_x(first, second[0] + second[1], w, p), axis=0))
+    for h in range(2):
+        snd4[h] = dot3([x_inv[k, h * NG : h * NG + NG, :] for k in range(2)], spectrum)
+        wide_send(7 + h, half(snd4, h), half(rx4, h))
 
     table_copies[5].wait()
-    wide_all(6, snd4, rx4).wait_recv()
-    parts = [
-        jnp.concatenate(exchange([rx4[c, pl.ds(j, NW, stride=8), :] for j in range(8)]), axis=0)
-        for c in range(2)
-    ]
-    snd5[0], snd5[1] = back((y_inv[0], y_inv[1]), parts[0], parts[1])
-    pencil_send(3, snd5, rx5)
+    for h in range(2):
+        wide_all(7 + h, half(snd4, h), half(rx4, h)).wait_recv()
+        parts = exchange([rx4[h, pl.ds(r, NW, stride=8), :] for r in range(8)])
+        sums = dot3((y_inv[0], y_inv[1]), split(jnp.concatenate(parts, axis=0)))
+        snd5[h] = combine(sums, 1.0)[0]
+        pencil_send(4 + h, half(snd5, h), half(rx5, h))
 
     table_copies[6].wait()
-    pencil_all(3, snd5, rx5).wait_recv()
-    halves_z = []
-    for c in range(2):
-        by_x = exchange([rx5[c, 32 * i : 32 * i + 32, :] for i in range(8)])
-        halves_z.append(
-            jnp.concatenate(
-                [by_x[cx][ty * 8 : ty * 8 + 8] for ty in range(4) for cx in range(8)], axis=0
-            )
+    lines = []
+    for h in range(2):
+        pencil_all(4 + h, half(snd5, h), half(rx5, h)).wait_recv()
+        lines.append(exchange([rx5[h, 32 * i : 32 * i + 32, :] for i in range(8)]))
+    lines = split(
+        jnp.concatenate(
+            [
+                jnp.concatenate(
+                    [
+                        lines[cx // 4][4 * c + cx % 4][ty * 8 : ty * 8 + 8]
+                        for ty in range(4)
+                        for cx in range(8)
+                    ],
+                    axis=0,
+                )
+                for c in range(2)
+            ],
+            axis=1,
         )
-    lines = split(jnp.concatenate(halves_z, axis=1))
+    )
     values = dot3(g_inv, lines, ((1,), (1,)))
     snd6[...] = pick_rows(values[: NW * 8], values[NW * 8 :], ty0, ty1).reshape(NW, 8, 128)
 
     def send_back(i):
         other = wide_peer(w, i)
-        wide_copy(7, snd6.at[other], rx6.at[w], other).start()
+        wide_copy(9, snd6.at[other], rx6.at[w], other).start()
 
     loop(NW - 1, send_back)
     rx6[w] = snd6[w]
     mesh = dot3(lines, (z_inv[0], z_inv[1]))
     for ty in range(4):
         for cx in range(8):
-            mesh_ref[cx, ty * 8 : ty * 8 + 8, :] = mesh[ty * 64 + cx * 8 : ty * 64 + cx * 8 + 8]
+            mesh_v[cx, ty * 8 : ty * 8 + 8, :] = mesh[ty * 64 + cx * 8 : ty * 64 + cx * 8 + 8]
+    mesh_copy = pltpu.make_async_copy(mesh_v, mesh_ref, pick_sem)
+    mesh_copy.start()
     ids_all.wait_send()
     for f in range(3):
         msg_all[f].wait_send()
+    for f in range(2):
         pencil_all(f, snd2.at[f], rx2.at[f]).wait_send()
-    for i in range(2):
-        wide_all(4 + i, snd3.at[i], rx3.at[i]).wait_send()
-    wide_all(6, snd4, rx4).wait_send()
-    pencil_all(3, snd5, rx5).wait_send()
-    wide_copy(7, snd6.at[others], rx6.at[others], (w + 1) % NW).wait()
-
-    lower = iota((8, 128), 1) < 64
+    wide_all(4, snd3.at[0], rx3.at[0]).wait_send()
+    for h in range(2):
+        pencil_all(2 + h, half(snd2.at[2], h), half(rx2.at[2], h)).wait_send()
+        wide_all(5 + h, half(snd3.at[1], h), half(rx3.at[1], h)).wait_send()
+        wide_all(7 + h, half(snd4, h), half(rx4, h)).wait_send()
+        pencil_all(4 + h, half(snd5, h), half(rx5, h)).wait_send()
+    wide_copy(9, snd6.at[others], rx6.at[others], (w + 1) % NW).wait()
 
     def read(b):
         o = owner[0, b]
-        here = jnp.where(pick[o, 0] == b, 0, 1)
-        tile_in = rx6[o]
-        side = jnp.where(lower, 0, 1)
-        tile_in = jnp.where(side == here, tile_in, 0.0)
+        pair = rx6[o]
+        here = jnp.where(pick[o, 0] == b, pair, roll(pair, 64, 1))
+        tile_in = here[:, :64]
         top = tile_in.astype(bf16).astype(f32)
         out = dot(jnp.concatenate([top, tile_in - top], axis=0).astype(bf16), spread[b])
         value = jnp.sum(jnp.where(kept(b), out[:8] + out[8:], 0.0), axis=0, keepdims=True)
         mass_ref[0:1, slots(b)] = value
 
     loop(NB, read, unroll=4)
+    mesh_copy.wait()
 
 
 def on_device(force_adjoint, paint_index, block_count, block_owner, block_tile):
@@ -511,7 +544,7 @@
             jax.ShapeDtypeStruct((1, NB * BP), f32),
         ),
         in_specs=[pl.BlockSpec(memory_space=pl.ANY)] * (5 + len(names)),
-        out_specs=(vmem, vmem),
+        out_specs=(pl.BlockSpec(memory_space=pl.ANY), vmem),
         scratch_shapes=[
             pltpu.VMEM((3, 1, NB * BP), f32),
             pltpu.VMEM((1, NB * BP), jnp.int32),
@@ -520,13 +553,13 @@
             pltpu.SMEM((1, NB), jnp.int32),
             pltpu.VMEM((1, NB), jnp.int32),
             *[pltpu.VMEM(t.shape, bf16) for t in tables],
-            pltpu.VMEM((NB, 128, BP), bf16),
+            pltpu.VMEM((NB, 64, BP), bf16),
             pltpu.VMEM((NB + 1, 3, 8, 128), f32),
             pltpu.VMEM((NW, 128), jnp.int32),
             pltpu.SMEM((NW, 128), jnp.int32),
-            pltpu.VMEM((NW, 2, 1, 128), jnp.int32),
+            pltpu.VMEM((NW, 1, 128), jnp.int32),
             pltpu.VMEM((3, NW, 8, 128), f32),
-            pltpu.VMEM((NW, 2, 1, 128), jnp.int32),
+            pltpu.VMEM((NW, 1, 128), jnp.int32),
             pltpu.VMEM((3, NW, 8, 128), f32),
             pltpu.VMEM((3, 2, NG, 128), f32),
             pltpu.VMEM((3, 2, NG, 128), f32),
@@ -535,7 +568,8 @@
             wave, wave, wave, wave,
             pltpu.VMEM((NW, 8, 128), f32),
             pltpu.VMEM((NW, 8, 128), f32),
-            dma((6,)), dma((7,)), dma, dma((8,)), dma((8,)), dma((4,)), dma((4,)),
+            pltpu.VMEM((8, 32, NG), f32),
+            dma((6,)), dma((7,)), dma, dma((10,)), dma((10,)), dma((6,)), dma((6,)),
         ],
         compiler_params=pltpu.CompilerParams(
             collective_id=0, has_side_effects=True, vmem_limit_bytes=60 << 20

time: 70.3 us -> 69.9 us (level)
  no operation moved by 1% of the time
where the time goes in v2:
time: 69.9 us; the launch traced here: 69.8 us
  Pallas kernels  66.8 us (96%)
  local copies, waits for them, and re-layouts  2.34 us (3%)
    pallas_call x1, Pallas kernels, on_device(): pl.pallas_call(step_kernel, out_shape=(jax.ShapeDtypeStruct((8, 32, NG),...  66.8 us
    unnamed x4, local copies, waits for them, and re-layouts  2.34 us

profile of v2, /device:TPU:1, one launch (start us, length us, event | category | flops | bytes accessed | tf_op | source)
XLA Modules:
  0.0 69.8 jit_solution(17068250443446822507)
XLA Ops:
  0.6 66.8 %step.1 = (f32[8,32,256]{2,1,0:T(8,128)}, f32[1,16384]{1,0:T(1,128)}) custom-call(f32[3,1,16384]{2,1,0:T(1,128)} %force_hbm.1, s32[1,16384]{1,0:T(1,128)} %cells_hbm.1, s32[1,32]{1,0:T(1,128)} %count_hbm.1, s32[1,32]{1,0:T(1,128)} %bitcast.1, s32[1,32]{1,0:T(1,128)} %tile_hbm.1, bf16[2,256,256]{2,1,0:T(8,128)(2,1)} %constant.14.clone.z_fwd_hbm, ...), custom_call_target="tpu_custom_call" | custom-call | tf_op jit(solution)/shard_map/step/pallas_call | solution.py:540
  67.4 0.0 copy-start
  67.4 1.7 %copy.16 = f32[8,32,256]{2,1,0:T(8,128)} copy(f32[8,32,256]{2,1,0:T(8,128)} %get-tuple-element.4) | data formatting | bytes 524288
  69.1 0.0 copy-done
  69.1 0.6 copy.17
Async XLA Ops:
  67.4 1.7 %copy-start = (f32[1,16384]{1,0:T(1,128)S(1)}, f32[1,16384]{1,0:T(1,128)}, u32[]{:S(2)}) copy-start(f32[1,16384]{1,0:T(1,128)} %get-tuple-element.5) | copy-start | bytes 196612

commit v3 on v2

--- a/solution.py
+++ b/solution.py
@@ -69,8 +69,7 @@
     c, s = waves(line, xt)
     x_fwd = np.concatenate([c, s], axis=0)
     c, s = waves(line, line)
-    full = np.stack([np.concatenate([c, -s], axis=1), np.concatenate([s, c], axis=1)])
-    x_inv = full.reshape(2, NW, 2, 4, 2 * NG).transpose(2, 1, 0, 3, 4).reshape(2 * NG, 2 * NG)
+    x_inv = np.concatenate([c, s], axis=0)
     return dict(
         z_fwd=halves(z_fwd),
         z_inv=halves(z_inv),
@@ -100,15 +99,17 @@
 
 
 def exchange(arrays):
-    chunk = iota(arrays[0].shape, 1) // 16
-    for b in range(3):
-        bit = (chunk >> b) & 1
+    lane = iota(arrays[0].shape, 1)
+    b = 1
+    while b < len(arrays):
+        bit = (lane // (8 * b)) & 1
         new = []
-        for i in range(8):
-            mine = (i >> b) & 1
-            shift = 16 << b if mine == 0 else 128 - (16 << b)
-            new.append(jnp.where(bit == mine, arrays[i], roll(arrays[i ^ (1 << b)], shift, 1)))
+        for i in range(len(arrays)):
+            mine = i // b % 2
+            shift = 8 * b if mine == 0 else 128 - 8 * b
+            new.append(jnp.where(bit == mine, arrays[i], roll(arrays[i ^ b], shift, 1)))
         arrays = new
+        b *= 2
     return arrays
 
 
@@ -163,34 +164,36 @@
     return out
 
 
-def solve_x(a, b, w, p):
-    cra, cia, sra, sia = a[:NG, :128], a[:NG, 128:], a[NG:, :128], a[NG:, 128:]
-    crb, cib, srb, sib = b[:NG, :128], b[:NG, 128:], b[NG:, :128], b[NG:, 128:]
+def solve_x(a, b, w, p, q):
     row = iota((NG, 128), 0)
     lane = iota((NG, 128), 1)
     signed = jnp.where(row < 128, row, row - NG)
     slope = jnp.where(row == 128, 0, signed).astype(f32)
-    p_re = slope * (cra + sia) + (crb + sib)
-    p_im = slope * (cia - sra) + (cib - srb)
-    q_re = (crb - sib) - slope * (cra - sia)
-    q_im = slope * (cia + sra) - (cib + srb)
-    alone = (w == 0) & ((lane & 63) < 16)
-    r_re = jnp.where(alone, q_re, roll(q_re, 64, 1))
-    r_im = jnp.where(alone, q_im, roll(q_im, 64, 1))
-    j = lane >> 4
+    sign = jnp.where(lane < 64, 1.0, -1.0)
+    cos_a, sin_a = sign * a[:NG], roll(a[NG:], 64, 1)
+    cos_b, sin_b = sign * b[:NG], roll(b[NG:], 64, 1)
+    here = sign * (slope * (cos_a + sin_a) + (cos_b + sin_b))
+    j = lane // 8 & 7
     base = 4 * w + (j & 3)
     ny = jnp.where((base == 0) & (j == 4), 128, base)
-    kz = lane & 15
-    nz = 16 * p + kz
+    nz = 16 * p + 8 * q + (lane & 7)
     flat = signed * signed + ny * ny
     factor = (1.0 / NG**2) / jnp.maximum(flat + nz * nz, 1).astype(f32)
+    if q:
+        return factor * here
+    there = (cos_b - sin_b) - slope * (cos_a - sin_a)
+    swapped = jnp.where((lane & 32) == 0, roll(there, 96, 1), roll(there, 32, 1))
+    there = jnp.where(base == 0, there, swapped)
     top = (1.0 / NG**2) / (flat + (NG // 2) ** 2).astype(f32)
-    shared = (nz == 0)
+    shared = nz == 0
     alpha = jnp.where(shared, 0.5 * (factor + top), factor)
     beta = jnp.where(shared, 0.5 * (top - factor), 0.0)
-    h_re = -(alpha * p_im + beta * r_im)
-    h_im = alpha * p_re + beta * r_re
-    return h_re, h_im
+    return alpha * here + beta * there
+
+
+def times_i(sums):
+    turned = roll(sums[:NG], 64, 1)
+    return jnp.where(iota((NG, 128), 1) < 64, -turned, turned) - sums[NG:]
 
 
 def wide_peer(w, i):
@@ -393,94 +396,93 @@
     ids0, ids1 = jnp.where(lower, pair, turned), jnp.where(lower, turned, pair)
     chosen = jnp.concatenate([one_hot_rows(ids0), one_hot_rows(ids1)], axis=0)
     table_copies[0].wait()
-    table_copies[1].wait()
     g_fwd = [dot(chosen, z_fwd[i]).astype(bf16) for i in range(2)]
-    g_inv = [dot(chosen, z_inv_t[i]).astype(bf16) for i in range(2)]
     ty0, ty1 = ids0 >> 5, ids1 >> 5
 
     kz = (iota((NG, 256), 1) & 127).astype(f32)
-    for f in range(3):
+
+    def z_lines(f):
         msg_all[f].wait_recv()
         field = msg_rx[f].reshape(NW * 8, 128)
         lines = dot3(split(scatter_rows(field, ty0, ty1)), g_fwd, ((0,), (0,)))
         if f == 2:
             lines = lines * kz
-        for h in range(2):
-            by_x = [
-                jnp.concatenate(
-                    [
-                        lines[ty * 64 + cx * 8 : ty * 64 + cx * 8 + 8, c * 128 : c * 128 + 128]
-                        for ty in range(4)
-                    ],
-                    axis=0,
-                )
-                for c in range(2)
-                for cx in range(4 * h, 4 * h + 4)
-            ]
-            for i, value in enumerate(exchange(by_x)):
-                snd2[f, h, 32 * i : 32 * i + 32, :] = value
-            if f == 2:
-                pencil_send(2 + h, half(snd2.at[f], h), half(rx2.at[f], h))
-        if f < 2:
-            pencil_send(f, snd2.at[f], rx2.at[f])
+        by_x = [
+            jnp.concatenate(
+                [
+                    lines[ty * 64 + cx * 8 : ty * 64 + cx * 8 + 8, c * 128 : c * 128 + 128]
+                    for ty in range(4)
+                ],
+                axis=0,
+            )
+            for c in range(2)
+            for cx in range(8)
+        ]
+        for i, value in enumerate(exchange(by_x)):
+            snd2[f, i % 2, i // 2 * 32 : i // 2 * 32 + 32, :] = value
+        if f == 1:
+            pencil_send(2, snd2.at[f], rx2.at[f])
+        else:
+            for q in range(2):
+                pencil_send(3 * f // 2 + q, half(snd2.at[f], q), half(rx2.at[f], q))
 
     slope = y_slopes()
+
+    def y_lines(f, q):
+        pencil_all(3 * f // 2 + q, half(snd2.at[f], q), half(rx2.at[f], q)).wait_recv()
+        return combine(dot3((y_fwd[0], y_fwd[1]), split(rx2[f, q])), -1.0)[0]
+
+    z_lines(0)
+    z_lines(1)
     table_copies[2].wait()
-    for f in range(2):
-        pencil_all(f, snd2.at[f], rx2.at[f]).wait_recv()
-        both = jnp.concatenate([rx2[f, 0], rx2[f, 1]], axis=1)
-        for h, value in enumerate(combine(dot3((y_fwd[0], y_fwd[1]), split(both)), -1.0)):
-            snd3[f, h] = value if f == 0 else slope * value
-        if f == 0:
-            wide_send(4, snd3.at[0], rx3.at[0])
-    for h in range(2):
-        pencil_all(2 + h, half(snd2.at[2], h), half(rx2.at[2], h)).wait_recv()
-        sums = dot3((y_fwd[0], y_fwd[1]), split(rx2[2, h]))
-        snd3[1, h] += combine(sums, -1.0)[0]
-        wide_send(5 + h, half(snd3.at[1], h), half(rx3.at[1], h))
+    snd3[0, 0] = y_lines(0, 0)
+    wide_send(4, half(snd3.at[0], 0), half(rx3.at[0], 0))
+    z_lines(2)
+    snd3[0, 1] = y_lines(0, 1)
+    wide_send(5, half(snd3.at[0], 1), half(rx3.at[0], 1))
+    table_copies[1].wait()
+    g_inv = [dot(chosen, z_inv_t[i]).astype(bf16) for i in range(2)]
+    pencil_all(2, snd2.at[1], rx2.at[1]).wait_recv()
+    both = jnp.concatenate([rx2[1, 0], rx2[1, 1]], axis=1)
+    for q, value in enumerate(combine(dot3((y_fwd[0], y_fwd[1]), split(both)), -1.0)):
+        snd3[1, q] = slope * value
+    for q in range(2):
+        snd3[1, q] += y_lines(2, q)
+        wide_send(6 + q, half(snd3.at[1], q), half(rx3.at[1], q))
 
     table_copies[3].wait()
     table_copies[4].wait()
 
-    def x_part(i, h):
-        parts = exchange([rx3[i, h, pl.ds(j, NW, stride=8), :] for j in range(8)])
-        parts = [jnp.concatenate(parts[c : c + 4], axis=0) for c in (0, 4)]
-        table = [x_fwd[k, :, h * 128 : h * 128 + 128] for k in range(2)]
-        return dot3(table, split(jnp.concatenate(parts, axis=1)))
-
-    wide_all(4, snd3.at[0], rx3.at[0]).wait_recv()
-    first = x_part(0, 0) + x_part(0, 1)
-    second = []
-    for h in range(2):
-        wide_all(5 + h, half(snd3.at[1], h), half(rx3.at[1], h)).wait_recv()
-        second.append(x_part(1, h))
-    spectrum = split(jnp.concatenate(solve_x(first, second[0] + second[1], w, p), axis=0))
-    for h in range(2):
-        snd4[h] = dot3([x_inv[k, h * NG : h * NG + NG, :] for k in range(2)], spectrum)
-        wide_send(7 + h, half(snd4, h), half(rx4, h))
+    def x_lines(i, q):
+        wide_all(4 + 2 * i + q, half(snd3.at[i], q), half(rx3.at[i], q)).wait_recv()
+        parts = exchange([rx3[i, q, pl.ds(j, NW, stride=8), :] for j in range(8)])
+        return jnp.concatenate(parts, axis=0)
+
+    both = jnp.concatenate([x_lines(0, 0), x_lines(0, 1)], axis=1)
+    first = dot3((x_fwd[0], x_fwd[1]), split(both))
+    for q in range(2):
+        second = dot3((x_fwd[0], x_fwd[1]), split(x_lines(1, q)))
+        solved = solve_x(first[:, q * 128 : q * 128 + 128], second, w, p, q)
+        snd4[q] = times_i(dot3((x_inv[0], x_inv[1]), split(solved)))
+        wide_send(8 + q, half(snd4, q), half(rx4, q))
 
     table_copies[5].wait()
-    for h in range(2):
-        wide_all(7 + h, half(snd4, h), half(rx4, h)).wait_recv()
-        parts = exchange([rx4[h, pl.ds(r, NW, stride=8), :] for r in range(8)])
+    for q in range(2):
+        wide_all(8 + q, half(snd4, q), half(rx4, q)).wait_recv()
+        parts = exchange([rx4[q, pl.ds(cx, NW, stride=8), :] for cx in range(8)])
         sums = dot3((y_inv[0], y_inv[1]), split(jnp.concatenate(parts, axis=0)))
-        snd5[h] = combine(sums, 1.0)[0]
-        pencil_send(4 + h, half(snd5, h), half(rx5, h))
+        snd5[q] = combine(sums, 1.0)[0]
+        pencil_send(5 + q, half(snd5, q), half(rx5, q))
 
     table_copies[6].wait()
-    lines = []
-    for h in range(2):
-        pencil_all(4 + h, half(snd5, h), half(rx5, h)).wait_recv()
-        lines.append(exchange([rx5[h, 32 * i : 32 * i + 32, :] for i in range(8)]))
+    for q in range(2):
+        pencil_all(5 + q, half(snd5, q), half(rx5, q)).wait_recv()
+    by_x = exchange([rx5[i % 2, i // 2 * 32 : i // 2 * 32 + 32, :] for i in range(16)])
     lines = split(
         jnp.concatenate(
             [
                 jnp.concatenate(
-                    [
-                        lines[cx // 4][4 * c + cx % 4][ty * 8 : ty * 8 + 8]
-                        for ty in range(4)
-                        for cx in range(8)
-                    ],
+                    [by_x[8 * c + cx][ty * 8 : ty * 8 + 8] for ty in range(4) for cx in range(8)],
                     axis=0,
                 )
                 for c in range(2)
@@ -493,7 +495,7 @@
 
     def send_back(i):
         other = wide_peer(w, i)
-        wide_copy(9, snd6.at[other], rx6.at[w], other).start()
+        wide_copy(10, snd6.at[other], rx6.at[w], other).start()
 
     loop(NW - 1, send_back)
     rx6[w] = snd6[w]
@@ -506,15 +508,15 @@
     ids_all.wait_send()
     for f in range(3):
         msg_all[f].wait_send()
-    for f in range(2):
-        pencil_all(f, snd2.at[f], rx2.at[f]).wait_send()
-    wide_all(4, snd3.at[0], rx3.at[0]).wait_send()
-    for h in range(2):
-        pencil_all(2 + h, half(snd2.at[2], h), half(rx2.at[2], h)).wait_send()
-        wide_all(5 + h, half(snd3.at[1], h), half(rx3.at[1], h)).wait_send()
-        wide_all(7 + h, half(snd4, h), half(rx4, h)).wait_send()
-        pencil_all(4 + h, half(snd5, h), half(rx5, h)).wait_send()
-    wide_copy(9, snd6.at[others], rx6.at[others], (w + 1) % NW).wait()
+    pencil_all(2, snd2.at[1], rx2.at[1]).wait_send()
+    for q in range(2):
+        for f in (0, 2):
+            pencil_all(3 * f // 2 + q, half(snd2.at[f], q), half(rx2.at[f], q)).wait_send()
+        for i in range(2):
+            wide_all(4 + 2 * i + q, half(snd3.at[i], q), half(rx3.at[i], q)).wait_send()
+        wide_all(8 + q, half(snd4, q), half(rx4, q)).wait_send()
+        pencil_all(5 + q, half(snd5, q), half(rx5, q)).wait_send()
+    wide_copy(10, snd6.at[others], rx6.at[others], (w + 1) % NW).wait()
 
     def read(b):
         o = owner[0, b]
@@ -569,7 +571,7 @@
             pltpu.VMEM((NW, 8, 128), f32),
             pltpu.VMEM((NW, 8, 128), f32),
             pltpu.VMEM((8, 32, NG), f32),
-            dma((6,)), dma((7,)), dma, dma((10,)), dma((10,)), dma((6,)), dma((6,)),
+            dma((6,)), dma((7,)), dma, dma((11,)), dma((11,)), dma((7,)), dma((7,)),
         ],
         compiler_params=pltpu.CompilerParams(
             collective_id=0, has_side_effects=True, vmem_limit_bytes=60 << 20

time: 69.9 us -> 68.1 us (0.974)
  Pallas kernels: 66.8 us -> 65 us
    pallas_call x1, Pallas kernels: 66.8 us -> 65 us  [on_device(): pl.pallas_call(step_kernel, out_shape=(jax.ShapeDtypeStruct((8, 32, NG),...]
where the time goes in v3:
time: 68.1 us; the launch traced here: 68 us
  Pallas kernels  65 us (95%)
  local copies, waits for them, and re-layouts  2.34 us (3%)
    pallas_call x1, Pallas kernels, on_device(): pl.pallas_call(step_kernel, out_shape=(jax.ShapeDtypeStruct((8, 32, NG),...  65 us
    unnamed x4, local copies, waits for them, and re-layouts  2.34 us

profile of v3, /device:TPU:1, one launch (start us, length us, event | category | flops | bytes accessed | tf_op | source)
XLA Modules:
  0.0 68.0 jit_solution(12188074554854289026)
XLA Ops:
  0.6 65.0 %step.1 = (f32[8,32,256]{2,1,0:T(8,128)}, f32[1,16384]{1,0:T(1,128)}) custom-call(f32[3,1,16384]{2,1,0:T(1,128)} %force_hbm.1, s32[1,16384]{1,0:T(1,128)} %cells_hbm.1, s32[1,32]{1,0:T(1,128)} %count_hbm.1, s32[1,32]{1,0:T(1,128)} %bitcast.1, s32[1,32]{1,0:T(1,128)} %tile_hbm.1, bf16[2,256,256]{2,1,0:T(8,128)(2,1)} %constant.14.clone.z_fwd_hbm, ...), custom_call_target="tpu_custom_call" | custom-call | tf_op jit(solution)/shard_map/step/pallas_call | solution.py:542
  65.6 0.0 copy-start
  65.6 1.7 %copy.16 = f32[8,32,256]{2,1,0:T(8,128)} copy(f32[8,32,256]{2,1,0:T(8,128)} %get-tuple-element.4) | data formatting | bytes 524288
  67.3 0.0 copy-done
  67.3 0.6 copy.17
Async XLA Ops:
  65.6 1.7 %copy-start = (f32[1,16384]{1,0:T(1,128)S(1)}, f32[1,16384]{1,0:T(1,128)}, u32[]{:S(2)}) copy-start(f32[1,16384]{1,0:T(1,128)} %get-tuple-element.5) | copy-start | bytes 196612

commit v4 on v3

--- a/solution.py
+++ b/solution.py
@@ -347,7 +347,7 @@
         out = out[:24] + out[24:]
         tiles[b] = jnp.concatenate([out, out], axis=1).reshape(3, 8, 128)
 
-    loop(NB, paint, unroll=4)
+    loop(NB, paint, unroll=16)
     pick_copy.wait()
     pl.semaphore_wait(barrier, NW - 1 + NP - 1)
 
@@ -404,7 +404,7 @@
     def z_lines(f):
         msg_all[f].wait_recv()
         field = msg_rx[f].reshape(NW * 8, 128)
-        lines = dot3(split(scatter_rows(field, ty0, ty1)), g_fwd, ((0,), (0,)))
+        lines = dot3(split(scatter_rows(field, ty0, ty1).T), g_fwd)
         if f == 2:
             lines = lines * kz
         by_x = [
@@ -434,12 +434,11 @@
 
     z_lines(0)
     z_lines(1)
+    z_lines(2)
     table_copies[2].wait()
-    snd3[0, 0] = y_lines(0, 0)
-    wide_send(4, half(snd3.at[0], 0), half(rx3.at[0], 0))
-    z_lines(2)
-    snd3[0, 1] = y_lines(0, 1)
-    wide_send(5, half(snd3.at[0], 1), half(rx3.at[0], 1))
+    for q in range(2):
+        snd3[0, q] = y_lines(0, q)
+        wide_send(4 + q, half(snd3.at[0], q), half(rx3.at[0], q))
     table_copies[1].wait()
     g_inv = [dot(chosen, z_inv_t[i]).astype(bf16) for i in range(2)]
     pencil_all(2, snd2.at[1], rx2.at[1]).wait_recv()
@@ -528,7 +527,7 @@
         value = jnp.sum(jnp.where(kept(b), out[:8] + out[8:], 0.0), axis=0, keepdims=True)
         mass_ref[0:1, slots(b)] = value
 
-    loop(NB, read, unroll=4)
+    loop(NB, read, unroll=16)
     mesh_copy.wait()
 
 

time: 68.1 us -> 64.8 us (0.952)
  Pallas kernels: 65 us -> 61.7 us
    pallas_call x1, Pallas kernels: 65 us -> 61.7 us  [on_device(): pl.pallas_call(step_kernel, out_shape=(jax.ShapeDtypeStruct((8, 32, NG),...]
where the time goes in v4:
time: 64.8 us; the launch traced here: 64.7 us
  Pallas kernels  61.7 us (95%)
  local copies, waits for them, and re-layouts  2.34 us (4%)
  between operations  0.65 us (1%)
    pallas_call x1, Pallas kernels, on_device(): pl.pallas_call(step_kernel, out_shape=(jax.ShapeDtypeStruct((8, 32, NG),...  61.7 us
    unnamed x4, local copies, waits for them, and re-layouts  2.34 us

profile of v4, /device:TPU:1, one launch (start us, length us, event | category | flops | bytes accessed | tf_op | source)
XLA Modules:
  0.0 64.7 jit_solution(17912435264587713576)
XLA Ops:
  0.6 61.7 %step.1 = (f32[8,32,256]{2,1,0:T(8,128)}, f32[1,16384]{1,0:T(1,128)}) custom-call(f32[3,1,16384]{2,1,0:T(1,128)} %force_hbm.1, s32[1,16384]{1,0:T(1,128)} %cells_hbm.1, s32[1,32]{1,0:T(1,128)} %count_hbm.1, s32[1,32]{1,0:T(1,128)} %bitcast.1, s32[1,32]{1,0:T(1,128)} %tile_hbm.1, bf16[2,256,256]{2,1,0:T(8,128)(2,1)} %constant.14.clone.z_fwd_hbm, ...), custom_call_target="tpu_custom_call" | custom-call | tf_op jit(solution)/shard_map/step/pallas_call | solution.py:541
  62.4 0.0 copy-start
  62.4 1.7 %copy.16 = f32[8,32,256]{2,1,0:T(8,128)} copy(f32[8,32,256]{2,1,0:T(8,128)} %get-tuple-element.4) | data formatting | bytes 524288
  64.1 0.0 copy-done
  64.1 0.6 copy.17
Async XLA Ops:
  62.4 1.7 %copy-start = (f32[1,16384]{1,0:T(1,128)S(1)}, f32[1,16384]{1,0:T(1,128)}, u32[]{:S(2)}) copy-start(f32[1,16384]{1,0:T(1,128)} %get-tuple-element.5) | copy-start | bytes 196612

commit v5 on v4

--- a/solution.py
+++ b/solution.py
@@ -49,16 +49,17 @@
     line = np.arange(NG)
     half = np.arange(NG // 2)
     sign = np.where(line % 2 == 0, 1.0, -1.0)
+    by_half = line.reshape(2, NP, 2, 8).transpose(2, 0, 1, 3).reshape(-1)
     c, s = waves(line, half)
     s = -s
     s[:, 0] = sign
-    z_fwd = np.concatenate([c, s], axis=1)
+    z_fwd = np.concatenate([c, s], axis=1)[:, by_half]
     c, s = waves(half, line)
     weight = np.where(half == 0, 1.0, 2.0)[:, None]
     c = c * weight
     s = -2.0 * s
     s[0] = sign
-    z_inv = np.concatenate([c, s], axis=0)
+    z_inv = np.concatenate([c, s], axis=0)[by_half]
     ky = ky_of_row()
     c, s = waves(ky, line)
     y_fwd = np.concatenate([c, s], axis=0)
@@ -91,6 +92,9 @@
 
 
 def dot3(a, b, dims=((1,), (0,))):
+    if b[0].shape[1] == 128:
+        high = dot(a[0], jnp.concatenate(b, axis=1))
+        return high[:, :128] + (high[:, 128:] + dot(a[1], b[0]))
     return dot(a[0], b[0], dims) + (dot(a[0], b[1], dims) + dot(a[1], b[0], dims))
 
 
@@ -399,7 +403,8 @@
     g_fwd = [dot(chosen, z_fwd[i]).astype(bf16) for i in range(2)]
     ty0, ty1 = ids0 >> 5, ids1 >> 5
 
-    kz = (iota((NG, 256), 1) & 127).astype(f32)
+    lane = iota((NG, 256), 1)
+    kz = ((lane // 8 & 7) * 16 + lane // 128 * 8 + (lane & 7)).astype(f32)
 
     def z_lines(f):
         msg_all[f].wait_recv()
@@ -407,24 +412,23 @@
         lines = dot3(split(scatter_rows(field, ty0, ty1).T), g_fwd)
         if f == 2:
             lines = lines * kz
-        by_x = [
-            jnp.concatenate(
-                [
-                    lines[ty * 64 + cx * 8 : ty * 64 + cx * 8 + 8, c * 128 : c * 128 + 128]
-                    for ty in range(4)
-                ],
-                axis=0,
-            )
-            for c in range(2)
-            for cx in range(8)
-        ]
-        for i, value in enumerate(exchange(by_x)):
-            snd2[f, i % 2, i // 2 * 32 : i // 2 * 32 + 32, :] = value
+        for q in range(2):
+            by_x = [
+                jnp.concatenate(
+                    [
+                        lines[ty * 64 + cx * 8 : ty * 64 + cx * 8 + 8, q * 128 : q * 128 + 128]
+                        for ty in range(4)
+                    ],
+                    axis=0,
+                )
+                for cx in range(8)
+            ]
+            for i, value in enumerate(exchange(by_x)):
+                snd2[f, q, 32 * i : 32 * i + 32, :] = value
+            if f != 1:
+                pencil_send(3 * f // 2 + q, half(snd2.at[f], q), half(rx2.at[f], q))
         if f == 1:
             pencil_send(2, snd2.at[f], rx2.at[f])
-        else:
-            for q in range(2):
-                pencil_send(3 * f // 2 + q, half(snd2.at[f], q), half(rx2.at[f], q))
 
     slope = y_slopes()
 
@@ -474,21 +478,18 @@
         pencil_send(5 + q, half(snd5, q), half(rx5, q))
 
     table_copies[6].wait()
+    lines = []
     for q in range(2):
         pencil_all(5 + q, half(snd5, q), half(rx5, q)).wait_recv()
-    by_x = exchange([rx5[i % 2, i // 2 * 32 : i // 2 * 32 + 32, :] for i in range(16)])
-    lines = split(
-        jnp.concatenate(
-            [
+        by_x = exchange([rx5[q, 32 * i : 32 * i + 32, :] for i in range(8)])
+        lines.append(
+            split(
                 jnp.concatenate(
-                    [by_x[8 * c + cx][ty * 8 : ty * 8 + 8] for ty in range(4) for cx in range(8)],
-                    axis=0,
+                    [by_x[cx][ty * 8 : ty * 8 + 8] for ty in range(4) for cx in range(8)], axis=0
                 )
-                for c in range(2)
-            ],
-            axis=1,
+            )
         )
-    )
+    lines = [jnp.concatenate([lines[0][i], lines[1][i]], axis=1) for i in range(2)]
     values = dot3(g_inv, lines, ((1,), (1,)))
     snd6[...] = pick_rows(values[: NW * 8], values[NW * 8 :], ty0, ty1).reshape(NW, 8, 128)
 
@@ -529,6 +530,22 @@
 
     loop(NB, read, unroll=16)
     mesh_copy.wait()
+
+
+def hand_over(mesh_in, mass_in, mesh_out, mass_out, mesh_v, mass_v, in_sem, out_sem):
+    reads = [pltpu.make_async_copy(mass_in, mass_v, in_sem.at[4])]
+    writes = [pltpu.make_async_copy(mass_v, mass_out, out_sem.at[4])]
+    for i in range(4):
+        part = pl.ds(2 * i, 2)
+        reads.append(pltpu.make_async_copy(mesh_in.at[part], mesh_v.at[part], in_sem.at[i]))
+        writes.append(pltpu.make_async_copy(mesh_v.at[part], mesh_out.at[part], out_sem.at[i]))
+    for copy in reads:
+        copy.start()
+    for read, write in zip(reads, writes):
+        read.wait()
+        write.start()
+    for copy in writes:
+        copy.wait()
 
 
 def on_device(force_adjoint, paint_index, block_count, block_owner, block_tile):
@@ -580,7 +597,21 @@
         force_adjoint, paint_index, block_count, block_owner.reshape(1, NB), block_tile,
         *[jnp.asarray(t) for t in tables],
     )
-    return mesh_grad, mass_grad
+    anywhere = pl.BlockSpec(memory_space=pl.ANY)
+    return pl.pallas_call(
+        hand_over,
+        out_shape=(
+            jax.ShapeDtypeStruct((8, 32, NG), f32),
+            jax.ShapeDtypeStruct((1, NB * BP), f32),
+        ),
+        in_specs=[anywhere, anywhere],
+        out_specs=(anywhere, anywhere),
+        scratch_shapes=[
+            pltpu.VMEM((8, 32, NG), f32), pltpu.VMEM((1, NB * BP), f32), dma((5,)), dma((5,)),
+        ],
+        compiler_params=pltpu.CompilerParams(vmem_limit_bytes=60 << 20),
+        name="hand_over",
+    )(mesh_grad, mass_grad)
 
 
 def solution(mesh):

time: 64.8 us -> 63.7 us (0.983)
  local copies, waits for them, and re-layouts: 2.34 us -> 0 us
  Pallas kernels: 61.7 us -> 62.9 us
    unnamed x4 -> x0, local copies, waits for them, and re-layouts: 2.34 us -> none
    pallas_call x0 -> x1, Pallas kernels: none -> 1.68 us  [on_device(): pl.pallas_call(hand_over, out_shape=(jax.ShapeDtypeStruct((8, 32, NG), f3...]
where the time goes in v5:
time: 63.7 us; the launch traced here: 63.6 us
  Pallas kernels  62.9 us (99%)
  between operations  0.64 us (1%)
    pallas_call x1, Pallas kernels, on_device(): pl.pallas_call(step_kernel, out_shape=(jax.ShapeDtypeStruct((8, 32, NG),...  61.3 us
    pallas_call x1, Pallas kernels, on_device(): pl.pallas_call(hand_over, out_shape=(jax.ShapeDtypeStruct((8, 32, NG), f3...  1.68 us

profile of v5, /device:TPU:1, one launch (start us, length us, event | category | flops | bytes accessed | tf_op | source)
XLA Modules:
  0.0 63.6 jit_solution(9297346234998767445)
XLA Ops:
  0.6 61.3 %step.1 = (f32[8,32,256]{2,1,0:T(8,128)}, f32[1,16384]{1,0:T(1,128)}) custom-call(f32[3,1,16384]{2,1,0:T(1,128)} %force_hbm.1, s32[1,16384]{1,0:T(1,128)} %cells_hbm.1, s32[1,32]{1,0:T(1,128)} %count_hbm.1, s32[1,32]{1,0:T(1,128)} %bitcast.1, s32[1,32]{1,0:T(1,128)} %tile_hbm.1, bf16[2,256,256]{2,1,0:T(8,128)(2,1)} %constant.14.clone.z_fwd_hbm, ...), custom_call_target="tpu_custom_call" | custom-call | tf_op jit(solution)/shard_map/step/pallas_call | solution.py:558
  61.9 1.7 %hand_over.1 = (f32[8,32,256]{2,1,0:T(8,128)}, f32[1,16384]{1,0:T(1,128)}) custom-call(f32[8,32,256]{2,1,0:T(8,128)} %get-tuple-element.4.mesh_in, f32[1,16384]{1,0:T(1,128)} %get-tuple-element.5.mass_in), custom_call_target="tpu_custom_call" | custom-call | tf_op jit(solution)/shard_map/hand_over/pallas_call | solution.py:601

commit v6 on v5

--- a/solution.py
+++ b/solution.py
@@ -294,7 +294,7 @@
             other = wide_peer(w, i)
             wide_copy(phase, rows(src, other, 8), rows(dst, w, 8), other).start()
 
-        loop(NW - 1, step)
+        loop(NW - 1, step, unroll=NW - 1)
         here = pl.ds(pl.multiple_of(w * 8, 8), 8)
         dst[:, here, :] = src[:, here, :]
 
@@ -307,7 +307,7 @@
             other = pencil_peer(p, i)
             pencil_copy(phase, rows(src, other, 32), rows(dst, p, 32), other).start()
 
-        loop(NP - 1, step)
+        loop(NP - 1, step, unroll=NP - 1)
         here = pl.ds(pl.multiple_of(p * 32, 32), 32)
         dst[:, here, :] = src[:, here, :]
 
@@ -374,7 +374,7 @@
         assemble(0, other)
         wide_copy(1, msg.at[0, other], msg_rx.at[0, w], other).start()
 
-    loop(NW - 1, send_first)
+    loop(NW - 1, send_first, unroll=NW - 1)
     for f in (1, 2):
 
         def send_field(i, f=f):
@@ -382,7 +382,7 @@
             assemble(f, other)
             wide_copy(1 + f, msg.at[f, other], msg_rx.at[f, w], other).start()
 
-        loop(NW - 1, send_field)
+        loop(NW - 1, send_field, unroll=NW - 1)
     number(w)
     ids_rx[w] = ids[w]
     for f in range(3):
@@ -497,7 +497,7 @@
         other = wide_peer(w, i)
         wide_copy(10, snd6.at[other], rx6.at[w], other).start()
 
-    loop(NW - 1, send_back)
+    loop(NW - 1, send_back, unroll=NW - 1)
     rx6[w] = snd6[w]
     mesh = dot3(lines, (z_inv[0], z_inv[1]))
     for ty in range(4):

time: 63.7 us -> 62.7 us (0.984)
  Pallas kernels: 62.9 us -> 61.9 us
    pallas_call x1, Pallas kernels: 61.3 us -> 60.2 us  [on_device(): pl.pallas_call(step_kernel, out_shape=(jax.ShapeDtypeStruct((8, 32, NG),...]
where the time goes in v6:
time: 62.7 us; the launch traced here: 62.6 us
  Pallas kernels  61.9 us (99%)
  between operations  0.64 us (1%)
    pallas_call x1, Pallas kernels, on_device(): pl.pallas_call(step_kernel, out_shape=(jax.ShapeDtypeStruct((8, 32, NG),...  60.2 us
    pallas_call x1, Pallas kernels, on_device(): pl.pallas_call(hand_over, out_shape=(jax.ShapeDtypeStruct((8, 32, NG), f3...  1.68 us

profile of v6, /device:TPU:1, one launch (start us, length us, event | category | flops | bytes accessed | tf_op | source)
XLA Modules:
  0.0 62.6 jit_solution(13655720794891861804)
XLA Ops:
  0.6 60.2 %step.1 = (f32[8,32,256]{2,1,0:T(8,128)}, f32[1,16384]{1,0:T(1,128)}) custom-call(f32[3,1,16384]{2,1,0:T(1,128)} %force_hbm.1, s32[1,16384]{1,0:T(1,128)} %cells_hbm.1, s32[1,32]{1,0:T(1,128)} %count_hbm.1, s32[1,32]{1,0:T(1,128)} %bitcast.1, s32[1,32]{1,0:T(1,128)} %tile_hbm.1, bf16[2,256,256]{2,1,0:T(8,128)(2,1)} %constant.14.clone.z_fwd_hbm, ...), custom_call_target="tpu_custom_call" | custom-call | tf_op jit(solution)/shard_map/step/pallas_call | solution.py:558
  60.9 1.7 %hand_over.1 = (f32[8,32,256]{2,1,0:T(8,128)}, f32[1,16384]{1,0:T(1,128)}) custom-call(f32[8,32,256]{2,1,0:T(8,128)} %get-tuple-element.4.mesh_in, f32[1,16384]{1,0:T(1,128)} %get-tuple-element.5.mass_in), custom_call_target="tpu_custom_call" | custom-call | tf_op jit(solution)/shard_map/hand_over/pallas_call | solution.py:601

commit v7 on v6

--- a/solution.py
+++ b/solution.py
@@ -353,7 +353,6 @@
 
     loop(NB, paint, unroll=16)
     pick_copy.wait()
-    pl.semaphore_wait(barrier, NW - 1 + NP - 1)
 
     left = iota((8, 128), 1) < 64
 
@@ -367,11 +366,17 @@
             name.append(jnp.where(b < NB, tile[0, jnp.minimum(b, NB - 1)], -1))
         ids[o] = jnp.where(iota((1, 128), 1) < 64, name[0], name[1])
 
+    def ready(o):
+        number(o)
+        for f in range(3):
+            assemble(f, o)
+
+    loop(NW, ready, unroll=NW)
+    pl.semaphore_wait(barrier, NW - 1 + NP - 1)
+
     def send_first(i):
         other = wide_peer(w, i)
-        number(other)
         wide_copy(0, ids.at[other], ids_rx.at[w], other).start()
-        assemble(0, other)
         wide_copy(1, msg.at[0, other], msg_rx.at[0, w], other).start()
 
     loop(NW - 1, send_first, unroll=NW - 1)
@@ -379,14 +384,11 @@
 
         def send_field(i, f=f):
             other = wide_peer(w, i)
-            assemble(f, other)
             wide_copy(1 + f, msg.at[f, other], msg_rx.at[f, w], other).start()
 
         loop(NW - 1, send_field, unroll=NW - 1)
-    number(w)
     ids_rx[w] = ids[w]
     for f in range(3):
-        assemble(f, w)
         msg_rx[f, w] = msg[f, w]
     others = pl.ds(0, NW - 1)
     ids_all = wide_copy(0, ids.at[others], ids_rx.at[others], (w + 1) % NW)

time: 62.7 us -> 62.3 us (level)
  no operation moved by 1% of the time
where the time goes in v7:
time: 62.3 us; the launch traced here: 62.1 us
  Pallas kernels  61.5 us (99%)
  between operations  0.64 us (1%)
    pallas_call x1, Pallas kernels, on_device(): pl.pallas_call(step_kernel, out_shape=(jax.ShapeDtypeStruct((8, 32, NG),...  59.8 us
    pallas_call x1, Pallas kernels, on_device(): pl.pallas_call(hand_over, out_shape=(jax.ShapeDtypeStruct((8, 32, NG), f3...  1.68 us

profile of v7, /device:TPU:1, one launch (start us, length us, event | category | flops | bytes accessed | tf_op | source)
XLA Modules:
  0.0 62.1 jit_solution(16081573181927802973)
XLA Ops:
  0.6 59.8 %step.1 = (f32[8,32,256]{2,1,0:T(8,128)}, f32[1,16384]{1,0:T(1,128)}) custom-call(f32[3,1,16384]{2,1,0:T(1,128)} %force_hbm.1, s32[1,16384]{1,0:T(1,128)} %cells_hbm.1, s32[1,32]{1,0:T(1,128)} %count_hbm.1, s32[1,32]{1,0:T(1,128)} %bitcast.1, s32[1,32]{1,0:T(1,128)} %tile_hbm.1, bf16[2,256,256]{2,1,0:T(8,128)(2,1)} %constant.14.clone.z_fwd_hbm, ...), custom_call_target="tpu_custom_call" | custom-call | tf_op jit(solution)/shard_map/step/pallas_call | solution.py:560
  60.4 1.7 %hand_over.1 = (f32[8,32,256]{2,1,0:T(8,128)}, f32[1,16384]{1,0:T(1,128)}) custom-call(f32[8,32,256]{2,1,0:T(8,128)} %get-tuple-element.4.mesh_in, f32[1,16384]{1,0:T(1,128)} %get-tuple-element.5.mass_in), custom_call_target="tpu_custom_call" | custom-call | tf_op jit(solution)/shard_map/hand_over/pallas_call | solution.py:603

commit v8 on v7

--- a/solution.py
+++ b/solution.py
@@ -267,12 +267,14 @@
         lambda i: pl.semaphore_signal(
             barrier, inc=1, device_id={"wide": wide_peer(w, i)}, device_id_type=MESH
         ),
+        unroll=NW - 1,
     )
     loop(
         NP - 1,
         lambda i: pl.semaphore_signal(
             barrier, inc=1, device_id={"pencil": pencil_peer(p, i)}, device_id_type=MESH
         ),
+        unroll=NP - 1,
     )
     for copy in table_copies:
         copy.start()
@@ -445,8 +447,6 @@
     for q in range(2):
         snd3[0, q] = y_lines(0, q)
         wide_send(4 + q, half(snd3.at[0], q), half(rx3.at[0], q))
-    table_copies[1].wait()
-    g_inv = [dot(chosen, z_inv_t[i]).astype(bf16) for i in range(2)]
     pencil_all(2, snd2.at[1], rx2.at[1]).wait_recv()
     both = jnp.concatenate([rx2[1, 0], rx2[1, 1]], axis=1)
     for q, value in enumerate(combine(dot3((y_fwd[0], y_fwd[1]), split(both)), -1.0)):
@@ -463,6 +463,8 @@
         parts = exchange([rx3[i, q, pl.ds(j, NW, stride=8), :] for j in range(8)])
         return jnp.concatenate(parts, axis=0)
 
+    table_copies[1].wait()
+    g_inv = [dot(chosen, z_inv_t[i]).astype(bf16) for i in range(2)]
     both = jnp.concatenate([x_lines(0, 0), x_lines(0, 1)], axis=1)
     first = dot3((x_fwd[0], x_fwd[1]), split(both))
     for q in range(2):

time: 62.3 us -> 63 us (1.011)
  Pallas kernels: 61.5 us -> 62.2 us
    pallas_call x1, Pallas kernels: 59.8 us -> 60.5 us  [on_device(): pl.pallas_call(step_kernel, out_shape=(jax.ShapeDtypeStruct((8, 32, NG),...]
where the time goes in v8:
time: 63 us; the launch traced here: 62.9 us
  Pallas kernels  62.2 us (99%)
  between operations  0.64 us (1%)
    pallas_call x1, Pallas kernels, on_device(): pl.pallas_call(step_kernel, out_shape=(jax.ShapeDtypeStruct((8, 32, NG),...  60.5 us
    pallas_call x1, Pallas kernels, on_device(): pl.pallas_call(hand_over, out_shape=(jax.ShapeDtypeStruct((8, 32, NG), f3...  1.68 us

profile of v8, /device:TPU:1, one launch (start us, length us, event | category | flops | bytes accessed | tf_op | source)
XLA Modules:
  0.0 62.9 jit_solution(11074406624991791438)
XLA Ops:
  0.6 60.5 %step.1 = (f32[8,32,256]{2,1,0:T(8,128)}, f32[1,16384]{1,0:T(1,128)}) custom-call(f32[3,1,16384]{2,1,0:T(1,128)} %force_hbm.1, s32[1,16384]{1,0:T(1,128)} %cells_hbm.1, s32[1,32]{1,0:T(1,128)} %count_hbm.1, s32[1,32]{1,0:T(1,128)} %bitcast.1, s32[1,32]{1,0:T(1,128)} %tile_hbm.1, bf16[2,256,256]{2,1,0:T(8,128)(2,1)} %constant.14.clone.z_fwd_hbm, ...), custom_call_target="tpu_custom_call" | custom-call | tf_op jit(solution)/shard_map/step/pallas_call | solution.py:562
  61.2 1.7 %hand_over.1 = (f32[8,32,256]{2,1,0:T(8,128)}, f32[1,16384]{1,0:T(1,128)}) custom-call(f32[8,32,256]{2,1,0:T(8,128)} %get-tuple-element.4.mesh_in, f32[1,16384]{1,0:T(1,128)} %get-tuple-element.5.mass_in), custom_call_target="tpu_custom_call" | custom-call | tf_op jit(solution)/shard_map/hand_over/pallas_call | solution.py:605
